TPU v7x, 32 devices: a whole 2x2x4 slice. The times are simulated.
32 devices in a mesh: groups: 2 (over y), coord: 8 (over z, x), ckpt: 2 (over core).
Axes of the slice: x: 2, y: 2, z: 4, core: 2. Of those that a mesh axis runs over, the one named last changes fastest.
Arguments:
- projection_input: bfloat16 [2, 2, 384, 4096], P('ckpt', 'groups', None, 'coord'), parts along dimension 1, may hold values from -6 to 6
- gate_output_gradient: bfloat16 [2, 2, 14336, 384], P('ckpt', 'groups', 'coord'), parts along dimension 1, may hold values from -0.59765625 to 0.59765625
- up_output_gradient: bfloat16 [2, 2, 14336, 384], P('ckpt', 'groups', 'coord'), parts along dimension 1, may hold values from -0.59765625 to 0.59765625
- hidden: bfloat16 [2, 2, 14336, 384], P('ckpt', 'groups', 'coord'), parts along dimension 1, may hold values from -6 to 6
- down_output_gradient: bfloat16 [2, 2, 384, 4096], P('ckpt', 'groups', None, 'coord'), parts along dimension 1, may hold values from -0.59765625 to 0.59765625
- gate_adapter_first: bfloat16 [2, 4096, 128], P('ckpt', 'coord'), may hold values from -0.09375 to 0.09375
- gate_adapter_second: bfloat16 [2, 14336, 128], P('ckpt', 'coord'), may hold values from -0.5 to 0.5
- up_adapter_first: bfloat16 [2, 4096, 128], P('ckpt', 'coord'), may hold values from -0.09375 to 0.09375
- up_adapter_second: bfloat16 [2, 14336, 128], P('ckpt', 'coord'), may hold values from -0.5 to 0.5
- down_adapter_first: bfloat16 [2, 14336, 128], P('ckpt', 'coord'), may hold values from -0.046875 to 0.046875
- down_adapter_second: bfloat16 [2, 4096, 128], P('ckpt', 'coord'), may hold values from -0.5 to 0.5
- random_sign_flags: int32 [16777216], P(('coord', 'ckpt')), may hold values 0 or 1
- sampled_coordinate_index: int32 [8192], replicated, may hold values from 0 to 16777215
Outputs:
- features: float32 [2, 8192], P('groups'), parts along dimension 0
There are 2 independent parts, one for each index of `groups`. A program takes and returns all parts, laid end to end along the dimension named above; an argument that names none is the same for every part. Nothing has to cross between parts.
All inputs are finite; a program needn't handle non-finite values. No bound on the sum of `random_sign_flags` on one device may be relied on, other than what follows from the above.
Results may differ from a plain program's by a relative error of at most 0.0031.
Values may be sent and summed in bfloat16 or wider, within the bound.
No kernel may reach another device: no remote copies, remote signals or barrier semaphores. Data moves between devices by JAX's collectives and lax.ppermute only.
A program may use at most 64 MiB of HBM per device.

v0:
```python
import functools

import jax
import jax.numpy as jnp
from jax import lax
from jax.experimental import pallas as pl
from jax.experimental.pallas import tpu as pltpu
from jax.sharding import PartitionSpec as P

F32 = jnp.float32
BF16 = jnp.bfloat16
MIB = 2**20
adapter_scale = 2.0

ANY = pl.BlockSpec(memory_space=pl.ANY)
VMEM = pl.BlockSpec(memory_space=pltpu.VMEM)
SMEM = pl.BlockSpec(memory_space=pltpu.SMEM)


def limit(size):
    return pltpu.CompilerParams(vmem_limit_bytes=int(size * MIB))


def in_hbm(value):
    return pltpu.with_memory_space_constraint(value, pltpu.HBM)


def exchange(value, axis, apart):
    pairs = [(source, source ^ apart) for source in range(lax.axis_size(axis))]
    return lax.ppermute(value, axis, pairs)


def dot(left, right, contract):
    return lax.dot_general(left, right, (contract, ((), ())), preferred_element_type=F32)


def fetch(sources, targets, sems, cuts):
    groups = []
    slot = 0
    for source, target, cut in zip(sources, targets, cuts, strict=True):
        rows = source.shape[0]
        size = -(-rows // (cut * 16)) * 16
        group = []
        for begin in range(0, rows, size):
            end = min(begin + size, rows)
            copy = pltpu.make_async_copy(
                source.at[begin:end], target.at[begin:end], sems.at[slot]
            )
            copy.start()
            group.append(copy)
            slot += 1
        groups.append(group)

    def wait(which):
        for copy in groups[which]:
            copy.wait()

    return wait


def stages_of(count):
    stages, shift = [], 0
    while count > 1:
        radix = 2 if shift == 0 else min(4, count)
        stages.append((shift, radix))
        shift += radix.bit_length() - 1
        count //= radix
    return stages


def my_digit(stage):
    return (lax.axis_index("coord") >> stage[0]) & (stage[1] - 1)


def hand_out(table, stage, own, sends):
    digit = my_digit(stage)
    size = own.shape[0]
    own[...] = table[pl.ds(pl.multiple_of(digit * size, 16), size), :]
    for step, send in enumerate(sends, 1):
        begin = pl.multiple_of((digit ^ step) * size, 16)
        send[...] = table[pl.ds(begin, size), :].astype(BF16)


def put_together(own, others, stage, table):
    digit = my_digit(stage)
    size = own.shape[0]
    table[pl.ds(pl.multiple_of(digit * size, 16), size), :] = own[...]
    for step, other in enumerate(others[::-1], 1):
        table[pl.ds(pl.multiple_of((digit ^ step) * size, 16), size), :] = other[...]


def handed_out(rows, rank, stage):
    size = rows // stage[1]
    sends = [jax.ShapeDtypeStruct((size, rank), BF16)] * (stage[1] - 1)
    return [jax.ShapeDtypeStruct((size, rank), F32)] + sends


def fill(table, row):
    if table.shape[0] > row:
        table[row:, :] = jnp.zeros((table.shape[0] - row, table.shape[1]), F32)


def short_kernel(stage, cuts, *refs):
    ins, (x, go), (own, *sends), (a_gate, a_up, b_down, table, sems) = (
        refs[:5], refs[5:7], refs[7:-5], refs[-5:]
    )
    wait = fetch(ins, (x, go, a_gate, a_up, b_down), sems, cuts)
    for which in range(5):
        wait(which)
    tokens = x.shape[0]
    table[:tokens, :] = dot(x[...], a_gate[...], ((1,), (0,)))
    table[tokens : 2 * tokens, :] = dot(x[...], a_up[...], ((1,), (0,)))
    table[2 * tokens : 3 * tokens, :] = dot(go[...], b_down[...], ((1,), (0,)))
    fill(table, 3 * tokens)
    hand_out(table, stage, own, sends)


def short_products(rows, stage, *ins):
    rank = ins[2].shape[1]
    cuts = (2, 2, 1, 1, 1)
    shapes = [jax.ShapeDtypeStruct(a.shape, a.dtype) for a in ins[:2]]
    shapes = shapes + handed_out(rows, rank, stage)
    x, go, *sends = pl.pallas_call(
        functools.partial(short_kernel, stage, cuts),
        out_shape=shapes,
        in_specs=[ANY] * len(ins),
        out_specs=[VMEM] * len(shapes),
        scratch_shapes=[pltpu.VMEM(a.shape, a.dtype) for a in ins[2:]]
        + [pltpu.VMEM((rows, rank), F32), pltpu.SemaphoreType.DMA((sum(cuts),))],
        compiler_params=limit(4),
        cost_estimate=pl.CostEstimate(flops=10**8, bytes_accessed=6 * 10**6, transcendentals=0),
        name="short",
    )(*ins)
    return x, go, sends


def long_kernel(stage, cut, *refs):
    ins, held, (own, *sends), (*adapters, table, sems) = refs[:6], refs[6:9], refs[9:-5], refs[-5:]
    rank = table.shape[1]
    per = cut + 1
    waits = []

    def begin(slot):
        wait = fetch(
            (ins[3 + slot], ins[slot]),
            (adapters[slot], held[slot]),
            sems.at[slot * per : (slot + 1) * per],
            (1, cut),
        )
        waits.append(wait)

    begin(0)
    begin(1)
    row = 0
    for slot in range(3):
        waits[slot](0)
        adapter = adapters[slot][...].T
        waits[slot](1)
        if slot == 0:
            begin(2)
        value = dot(adapter, held[slot][...], ((1,), (0,)))
        for part in range(value.shape[1] // rank):
            table[row : row + rank, :] = value[:, part * rank : (part + 1) * rank]
            row += rank
    fill(table, row)
    hand_out(table, stage, own, sends)


def long_products(rows, stage, *ins):
    rank = ins[3].shape[1]
    cut = 4
    held = [jax.ShapeDtypeStruct(a.shape, a.dtype) for a in ins[:3]]
    shapes = held + handed_out(rows, rank, stage)
    outs = pl.pallas_call(
        functools.partial(long_kernel, stage, cut),
        out_shape=shapes,
        in_specs=[ANY] * 6,
        out_specs=[VMEM] * len(shapes),
        scratch_shapes=[pltpu.VMEM(a.shape, a.dtype) for a in ins[3:]]
        + [pltpu.VMEM((rows, rank), F32), pltpu.SemaphoreType.DMA((3 * (cut + 1),))],
        compiler_params=limit(6),
        cost_estimate=pl.CostEstimate(flops=10**9, bytes_accessed=8 * 10**6, transcendentals=0),
        name="long",
    )(*ins)
    return *outs[:3], outs[3:]


def add_kernel(following, count, *refs):
    total = refs[0][...]
    for got in refs[1 : 1 + count]:
        total = total + got[...].astype(F32)
    if following is None:
        refs[1 + count][...] = total.astype(BF16)
    else:
        outs, table = refs[1 + count : -1], refs[-1]
        table[...] = total
        hand_out(table, following, outs[0], outs[1:])


def add_up(own, got, following):
    if following is None:
        shapes, scratch = [jax.ShapeDtypeStruct(own.shape, BF16)], []
    else:
        shapes, scratch = handed_out(*own.shape, following), [pltpu.VMEM(own.shape, F32)]
    return pl.pallas_call(
        functools.partial(add_kernel, following, len(got)),
        out_shape=shapes,
        in_specs=[VMEM] * (1 + len(got)),
        out_specs=[VMEM] * len(shapes),
        scratch_shapes=scratch,
        compiler_params=limit(3),
        name="add_up",
    )(own, *got)


def join_kernel(stage, own, *refs):
    put_together(own, refs[:-1], stage, refs[-1])


def join(own, got, stage):
    return pl.pallas_call(
        functools.partial(join_kernel, stage),
        out_shape=jax.ShapeDtypeStruct((own.shape[0] * stage[1], own.shape[1]), BF16),
        in_specs=[VMEM] * (1 + len(got)),
        out_specs=VMEM,
        compiler_params=limit(3),
        name="join",
    )(own, *got)


def swap(sends, stage):
    return [
        exchange(sends[step - 1], "coord", step << stage[0]) for step in range(stage[1] - 1, 0, -1)
    ]


def after(first, second):
    return lax.optimization_barrier((first, second))[1]


def all_sums(halves, stages, ahead):
    beside = []
    owns = [half[0] for half in halves]
    sends = [half[1:] for half in halves]
    for stage, following in zip(stages, stages[1:] + [None], strict=True):
        got = [swap(send, stage) for send in sends]
        for i in range(len(owns)):
            own = after(owns[0], owns[i]) if i else owns[i]
            order = got[i][1:] + got[i][:1] if i else got[i]
            owns[i], *sends[i] = add_up(own, order, following)
    for stage in stages[:0:-1]:
        got = [swap([own] * (stage[1] - 1), stage) for own in owns]
        for i in range(len(owns)):
            own = after(owns[0], owns[i]) if i else owns[i]
            if stage is stages[1]:
                beside.append(ahead[i](owns[0]))
                own = after(beside[i], own)
            owns[i] = join(own, got[i], stage)
    return beside, [[own] + swap([own] * (stages[0][1] - 1), stages[0]) for own in owns]


def total_over(contrib, count):
    assert lax.axis_size("ckpt") == 2
    core = lax.axis_index("ckpt")
    total = contrib + exchange(contrib, "ckpt", 1)
    shift = 0
    while 1 << shift < count:
        radix = min(8, count >> shift)
        half = radix // 2
        terms = []
        for step in range(half):
            nearer, further = (step or half) << shift, (half + step) << shift
            pairs = [(2 * c + 1, 2 * (c ^ nearer)) for c in range(count)]
            pairs += [(2 * c, 2 * (c ^ further) + 1) for c in range(count)]
            got = lax.ppermute(total, ("coord", "ckpt"), pairs)
            terms.append(got if step else jnp.where(core == 0, total, got))
        while len(terms) > 1:
            terms = [a + b for a, b in zip(terms[::2], terms[1::2], strict=True)]
        total = terms[0] + exchange(terms[0], "ckpt", 1)
        shift += radix.bit_length() - 1
    return total


def turn_kernel(x, go, x_t, go_t):
    x_t[...] = x[...].T
    go_t[...] = go[...].T


def turn(x, go):
    shape = jax.ShapeDtypeStruct(x.shape[::-1], BF16)
    return pl.pallas_call(
        turn_kernel,
        out_shape=[shape, shape],
        in_specs=[VMEM, VMEM],
        out_specs=[VMEM, VMEM],
        compiler_params=limit(4),
        name="turn",
    )(x, go)


def butterflies(blocks):
    half = 1
    while half < len(blocks):
        done = list(blocks)
        for low in range(len(blocks)):
            if not low & half:
                a, b = blocks[low], blocks[low | half]
                if b is None:
                    done[low], done[low | half] = a, a
                else:
                    done[low], done[low | half] = a + b, a - b
        blocks, half = done, half * 2
    return blocks


def along_block(value, out, row):
    size = value.shape[0]
    tiles = butterflies([value[i : i + 8, :] for i in range(0, size, 8)])
    for i, tile in enumerate(tiles):
        out[row + 8 * i : row + 8 * i + 8, :] = tile
    for begin in range(row, row + size, 64):
        tiles = butterflies([out[pl.ds(begin + j, 8, stride=8), :] for j in range(8)])
        for j, tile in enumerate(tiles):
            out[begin + 8 * j : begin + 8 * j + 8, :] = tile


def signed(value, flags, row):
    return jnp.where(flags[row : row + value.shape[0], :] == 0, value, -value)


def keep(aligned, value, flags, row, out):
    value = signed(value, flags, row)
    if aligned:
        along_block(value, out, row)
    else:
        out[row : row + value.shape[0], :] = value


def wide_kernel(aligned, block, first, stage, *refs):
    parts, refs = refs[: stage[1]], refs[stage[1] :]
    gg, gu, h, flags, out, table = refs
    put_together(parts[0], parts[1:], stage, table)
    tokens = gg.shape[1]
    flags = flags.at[first : first + out.shape[0]]
    row = 0
    for slot, piece in enumerate((gg, gu, h)):
        product = table[slot * tokens : (slot + 1) * tokens, :]
        size = block if aligned else piece.shape[0]
        for begin in range(0, piece.shape[0], size):
            value = dot(piece[begin : begin + size, :], product, ((1,), (0,)))
            keep(aligned, value, flags, row, out)
            row += size


def wide(aligned, block, first, stage, parts, gg, gu, h, flags):
    rank = flags.shape[1]
    return pl.pallas_call(
        functools.partial(wide_kernel, aligned, block, first, stage),
        out_shape=jax.ShapeDtypeStruct((3 * gg.shape[0], rank), F32),
        in_specs=[VMEM] * (len(parts) + 4),
        out_specs=VMEM,
        scratch_shapes=[pltpu.VMEM((parts[0].shape[0] * stage[1], rank), BF16)],
        compiler_params=limit(6),
        cost_estimate=pl.CostEstimate(flops=10**9, bytes_accessed=10**7, transcendentals=0),
        name="wide",
    )(*parts, gg, gu, h, flags)


def rows_kernel(aligned, block, stage, *refs):
    parts, refs = refs[: stage[1]], refs[stage[1] :]
    x_t, go_t, wide_mix, flags, mix, table = refs
    width, tokens = x_t.shape
    first = 3 * width
    length, rank = mix.shape
    put_together(parts[0], parts[1:], stage, table)
    product = [
        jnp.concatenate(
            [table[slot * tokens + part : slot * tokens + part + rank, :] for part in range(0, tokens, rank)],
            axis=1,
        )
        for slot in range(3)
    ]
    size = block if aligned else width
    both = jnp.concatenate(product[:2], axis=0)
    for begin in range(0, width, size):
        value = dot(x_t[begin : begin + size, :], both, ((1,), (1,)))
        keep(aligned, value[:, :rank], flags, begin, mix)
        keep(aligned, value[:, rank:], flags, width + begin, mix)
        value = dot(go_t[begin : begin + size, :], product[2], ((1,), (1,)))
        keep(aligned, value, flags, 2 * width + begin, mix)
    filled = first + wide_mix.shape[0]
    if not aligned:
        mix[first:filled, :] = wide_mix[...]
        mix[filled:, :] = jnp.zeros((length - filled, rank), F32)
        for begin in range(0, length, block):
            along_block(mix[begin : begin + block, :], mix, begin)
    number = length // block
    full = -(-filled // block)

    def load(i, begin):
        if not aligned or i * block < first:
            return mix[pl.ds(i * block + begin, 8), :]
        if i >= full:
            return None
        return wide_mix[pl.ds(i * block - first + begin, 8), :]

    def across(step, _):
        begin = pl.multiple_of(step * 8, 8)
        for i, value in enumerate(butterflies([load(i, begin) for i in range(number)])):
            mix[pl.ds(i * block + begin, 8), :] = value
        return _

    if number > 1:
        lax.fori_loop(0, block // 8, across, 0, unroll=4)


def along_rows(aligned, block, stage, length, parts, x_t, go_t, wide_mix, flags):
    rank = flags.shape[1]
    return pl.pallas_call(
        functools.partial(rows_kernel, aligned, block, stage),
        out_shape=jax.ShapeDtypeStruct((length, rank), F32),
        in_specs=[VMEM] * (len(parts) + 4),
        out_specs=VMEM,
        scratch_shapes=[pltpu.VMEM((parts[0].shape[0] * stage[1], rank), BF16)],
        compiler_params=limit(6),
        name="along_rows",
    )(*parts, x_t, go_t, wide_mix, flags)


def parity(value):
    for fold in (16, 8, 4, 2, 1):
        value = value ^ (value >> fold)
    return value & 1


def signs_kernel(bits, lanes, out):
    rank = out.shape[0]
    device = lax.axis_index("coord") * lax.axis_size("ckpt") + lax.axis_index("ckpt")
    index = lanes[...]

    def sign(bit):
        return (1 - 2 * (bit & 1)).astype(F32)

    low = lax.broadcasted_iota(jnp.int32, (8, index.shape[1]), 0)
    tile = sign(parity((index >> bits) & device))
    for bit in range(3):
        tile = tile * jnp.where((low >> bit & 1) == 0, 1.0, sign(index >> bit))
    tiles = [tile]
    for bit in range(3, rank.bit_length() - 1):
        tiles = tiles + [tile * sign(index >> bit) for tile in tiles]
    out[...] = jnp.concatenate(tiles, axis=0).astype(BF16)


def signs_of(rank, bits, index):
    samples = index.shape[0]
    return pl.pallas_call(
        functools.partial(signs_kernel, bits),
        out_shape=jax.ShapeDtypeStruct((rank, samples), BF16),
        in_specs=[VMEM],
        out_specs=VMEM,
        compiler_params=limit(10),
        name="signs",
    )(index.reshape(1, samples))


def pick_kernel(mix, where, rows):
    samples = rows.shape[0]
    unroll, ahead = min(256, samples), 16

    def pick(step, _):
        begin = step * unroll
        held = []
        for i in range(unroll):
            held.append(mix[where[begin + i]])
            if i >= ahead:
                rows[begin + i - ahead] = held[i - ahead]
        for i in range(unroll - ahead, unroll):
            rows[begin + i] = held[i]
        return _

    lax.fori_loop(0, samples // unroll, pick, 0)


def picked(mix, where):
    rank, samples = mix.shape[1], where.shape[0]
    rows = pl.pallas_call(
        pick_kernel,
        out_shape=jax.ShapeDtypeStruct((samples, 1, rank), F32),
        in_specs=[VMEM, SMEM],
        out_specs=VMEM,
        compiler_params=limit(4),
        name="picked",
    )(mix.reshape(-1, 1, rank), where)
    return rows.reshape(samples, rank)


def sample_kernel(final_scale, rows, signs, out):
    samples, rank = rows.shape
    shape = (rank, rank)
    diagonal = lax.broadcasted_iota(jnp.int32, shape, 0) == lax.broadcasted_iota(jnp.int32, shape, 1)
    for begin in range(0, samples, rank):
        value = rows[begin : begin + rank, :]
        high = value.astype(BF16)
        low = (value - high.astype(F32)).astype(BF16)
        sign = signs[:, begin : begin + rank]
        mixed = dot(
            jnp.concatenate([high, low], axis=1), jnp.concatenate([sign, sign], axis=0), ((1,), (0,))
        )
        chosen = jnp.sum(jnp.where(diagonal, mixed, 0.0), axis=0, keepdims=True)
        out[:, begin : begin + rank] = chosen * final_scale


def sampled(final_scale, rows, signs):
    return pl.pallas_call(
        functools.partial(sample_kernel, final_scale),
        out_shape=jax.ShapeDtypeStruct((1, rows.shape[0]), F32),
        in_specs=[VMEM, VMEM],
        out_specs=VMEM,
        compiler_params=limit(4),
        name="sampled",
    )(rows, signs)


def shards(x, gg, gu, h, go, a_gate, b_gate, a_up, b_up, a_down, b_down, flags, index):
    x, go, gg, gu, h = [a[0, 0] for a in (x, go, gg, gu, h)]
    a_gate, b_gate, a_up, b_up, a_down, b_down = [
        a[0] for a in (a_gate, b_gate, a_up, b_up, a_down, b_down)
    ]
    count = lax.axis_size("coord")
    tokens, rank = x.shape[0], a_gate.shape[1]
    total = flags.shape[0] * count * lax.axis_size("ckpt")
    flags = flags.reshape(-1, rank)
    length = flags.shape[0]
    first = 3 * x.shape[1]
    block = min(256, length)
    aligned = x.shape[1] % block == 0 and gg.shape[0] % block == 0
    where = (index >> (rank.bit_length() - 1)) & (length - 1)
    where = (where & ~63) | (where & 7) << 3 | where >> 3 & 7
    stages = stages_of(count)
    rows = 16 * count * -(-3 * tokens // (16 * count))
    x, go, short = short_products(
        rows, stages[0], *[in_hbm(a) for a in (x, go, a_gate, a_up, b_down)]
    )
    gg, gu, h, long = long_products(
        rows, stages[0], *[in_hbm(a) for a in (gg, gu, h, b_gate, b_up, a_down)]
    )
    flags = after(long[0], flags)
    bits = (length * rank).bit_length() - 1
    ahead = (
        lambda ready: turn(x, go),
        lambda ready: signs_of(rank, bits, after(ready, index)),
    )
    ((x_t, go_t), signs), (short, long) = all_sums([short, long], stages, ahead)
    wide_mix = wide(aligned, block, first, stages[0], short, gg, gu, h, flags)
    final_scale = adapter_scale * float(total) ** -0.5
    mix = along_rows(aligned, block, stages[0], length, long, x_t, go_t, wide_mix, flags)
    contrib = sampled(final_scale, picked(mix, where), signs)
    return total_over(contrib, count)


def solution(mesh):
    in_specs = (
        P("ckpt", "groups", None, "coord"),
        P("ckpt", "groups", "coord", None),
        P("ckpt", "groups", "coord", None),
        P("ckpt", "groups", "coord", None),
        P("ckpt", "groups", None, "coord"),
        P("ckpt", "coord", None),
        P("ckpt", "coord", None),
        P("ckpt", "coord", None),
        P("ckpt", "coord", None),
        P("ckpt", "coord", None),
        P("ckpt", "coord", None),
        P(("coord", "ckpt")),
        P(),
    )
    out_specs = P("groups", None)
    return jax.shard_map(shards, mesh=mesh, in_specs=in_specs, out_specs=out_specs, check_vma=False)
```

profile of v0, /device:TPU:0, one launch (start us, length us, event | category | flops | bytes accessed | tf_op | source)
XLA Modules:
  0.0 60.0 jit_solution(7048989335825420679)
XLA Ops:
  0.0 1.9 %short.1 = (bf16[384,512]{1,0:T(8,128)(2,1)S(1)}, bf16[384,512]{1,0:T(8,128)(2,1)S(1)}, f32[576,128]{1,0:T(8,128)S(1)}, bf16[576,128]{1,0:T(8,128)(2,1)S(1)}) custom-call(bf16[384,512]{1,0:T(8,128)(2,1)} %bitcast.26, bf16[384,512]{1,0:T(8,128)(2,1)} %bitcast.27, bf16[512,128]{1,0:T(8,128)(2,1)} %bitcast.28, bf16[512,128]{1,0:T(8,128)(2,1)} %bitcast.29, ...), custom_call_target="tpu_custom_call" | custom-call | flops 100000000 | bytes 6000000 | tf_op jit(solution)/shard_map/short/pallas_call | solution.py:123
  1.9 3.1 %collective-permute-start = (bf16[576,128]{1,0:T(8,128)(2,1)S(1)}, bf16[576,128]{1,0:T(8,128)(2,1)S(1)}, u32[]{:S(2)}, u32[]{:S(2)}) collective-permute-start(bf16[576,128]{1,0:T(8,128)(2,1)S(1)} %get-tuple-element.36), channel_id=1, source_target_pairs={{0,2},{2,0},{4,6},{6,4},{8,10},{10,8},{12,14},{14,12},{1,3},{3,1},... | collective-permute-start | bytes 442376 | tf_op jit(solution)/shard_map/ppermute | solution.py:30
  5.0 3.8 %long.1 = (bf16[1792,384]{1,0:T(8,128)(2,1)S(1)}, bf16[1792,384]{1,0:T(8,128)(2,1)S(1)}, bf16[1792,384]{1,0:T(8,128)(2,1)S(1)}, f32[576,128]{1,0:T(8,128)S(1)}, bf16[576,128]{1,0:T(8,128)(2,1)S(1)}) custom-call(bf16[1792,384]{1,0:T(8,128)(2,1)} %bitcast.20, bf16[1792,384]{1,0:T(8,128)(2,1)} %bitcast.21, bf16[1792,384]{1,0:T(8,128)(2,1)} %bitcast.22, ...), custom_call_target="tpu_custom_call" | custom-call | flops 1000000000 | bytes 8000000 | tf_op jit(solution)/shard_map/long/pallas_call | solution.py:174
  8.7 0.0 copy-start.1
  8.8 0.1 collective-permute-start.7
  8.9 0.0 collective-permute-done.refs_1_
  8.9 4.1 %collective-permute-start.1 = (bf16[144,128]{1,0:T(8,128)(2,1)S(1)}, bf16[144,128]{1,0:T(8,128)(2,1)S(1)}, u32[]{:S(2)}, u32[]{:S(2)}) collective-permute-start(bf16[144,128]{1,0:T(8,128)(2,1)S(1)} %get-tuple-element.38), channel_id=1, source_target_pairs={{0,12},{2,14},{4,8},{6,10},{8,4},{10,6},{12,0},{14,2},{1,13},{3,15... | collective-permute-start | bytes 110600 | tf_op jit(solution)/shard_map/ppermute | solution.py:30
  13.1 0.0 collective-permute-start.2
  13.1 0.6 %collective-permute-start.3 = (bf16[144,128]{1,0:T(8,128)(2,1)S(1)}, bf16[144,128]{1,0:T(8,128)(2,1)S(1)}, u32[]{:S(2)}, u32[]{:S(2)}) collective-permute-start(bf16[144,128]{1,0:T(8,128)(2,1)S(1)} %get-tuple-element.40), channel_id=1, source_target_pairs={{0,4},{2,6},{4,0},{6,2},{8,12},{10,14},{12,8},{14,10},{1,5},{3,7},... | collective-permute-start | bytes 110600 | tf_op jit(solution)/shard_map/ppermute | solution.py:30
  13.7 0.4 collective-permute-done.7.refs_1_
  14.1 0.0 copy-start
  14.2 3.7 %collective-permute-start.10 = (bf16[144,128]{1,0:T(8,128)(2,1)S(1)}, bf16[144,128]{1,0:T(8,128)(2,1)S(1)}, u32[]{:S(2)}, u32[]{:S(2)}) collective-permute-start(bf16[144,128]{1,0:T(8,128)(2,1)S(1)} %get-tuple-element.50), channel_id=1, source_target_pairs={{0,12},{2,14},{4,8},{6,10},{8,4},{10,6},{12,0},{14,2},{1,13},{3,15... | collective-permute-start | bytes 110600 | tf_op jit(solution)/shard_map/ppermute | solution.py:30
  17.8 0.0 collective-permute-start.8
  17.8 0.0 collective-permute-done.1.refs_1_
  17.9 0.8 %collective-permute-start.9 = (bf16[144,128]{1,0:T(8,128)(2,1)S(1)}, bf16[144,128]{1,0:T(8,128)(2,1)S(1)}, u32[]{:S(2)}, u32[]{:S(2)}) collective-permute-start(bf16[144,128]{1,0:T(8,128)(2,1)S(1)} %get-tuple-element.49), channel_id=1, source_target_pairs={{0,4},{2,6},{4,0},{6,2},{8,12},{10,14},{12,8},{14,10},{1,5},{3,7},... | collective-permute-start | bytes 110600 | tf_op jit(solution)/shard_map/ppermute | solution.py:30
  18.6 0.0 collective-permute-done.2.refs_2_
  18.6 0.0 collective-permute-done.3.refs_3_
  18.7 3.7 %collective-permute-start.4 = (bf16[144,128]{1,0:T(8,128)(2,1)S(1)}, bf16[144,128]{1,0:T(8,128)(2,1)S(1)}, u32[]{:S(2)}, u32[]{:S(2)}) collective-permute-start(bf16[144,128]{1,0:T(8,128)(2,1)S(1)} %add_up.5.own), channel_id=1, source_target_pairs={{0,12},{2,14},{4,8},{6,10},{8,4},{10,6},{12,0},{14,2},{1,13},{3,15... | collective-permute-start | bytes 110600 | tf_op jit(solution)/shard_map/ppermute | solution.py:30
  22.3 0.0 collective-permute-start.5
  22.3 0.0 collective-permute-done.10.refs_3_
  22.3 0.8 %collective-permute-start.6 = (bf16[144,128]{1,0:T(8,128)(2,1)S(1)}, bf16[144,128]{1,0:T(8,128)(2,1)S(1)}, u32[]{:S(2)}, u32[]{:S(2)}) collective-permute-start(bf16[144,128]{1,0:T(8,128)(2,1)S(1)} %add_up.5.own), channel_id=1, source_target_pairs={{0,4},{2,6},{4,0},{6,2},{8,12},{10,14},{12,8},{14,10},{1,5},{3,7},... | collective-permute-start | bytes 110600 | tf_op jit(solution)/shard_map/ppermute | solution.py:30
  23.1 0.0 collective-permute-done.8.refs_1_
  23.1 0.0 collective-permute-done.9.refs_2_
  23.2 3.7 %collective-permute-start.11 = (bf16[144,128]{1,0:T(8,128)(2,1)S(1)}, bf16[144,128]{1,0:T(8,128)(2,1)S(1)}, u32[]{:S(2)}, u32[]{:S(2)}) collective-permute-start(bf16[144,128]{1,0:T(8,128)(2,1)S(1)} %add_up.7.own), channel_id=1, source_target_pairs={{0,12},{2,14},{4,8},{6,10},{8,4},{10,6},{12,0},{14,2},{1,13},{3,15... | collective-permute-start | bytes 110600 | tf_op jit(solution)/shard_map/ppermute | solution.py:30
  26.8 0.0 collective-permute-start.12
  26.8 0.0 collective-permute-done.4.refs_0_
  26.8 0.8 %collective-permute-start.13 = (bf16[144,128]{1,0:T(8,128)(2,1)S(1)}, bf16[144,128]{1,0:T(8,128)(2,1)S(1)}, u32[]{:S(2)}, u32[]{:S(2)}) collective-permute-start(bf16[144,128]{1,0:T(8,128)(2,1)S(1)} %add_up.7.own), channel_id=1, source_target_pairs={{0,4},{2,6},{4,0},{6,2},{8,12},{10,14},{12,8},{14,10},{1,5},{3,7},... | collective-permute-start | bytes 110600 | tf_op jit(solution)/shard_map/ppermute | solution.py:30
  27.6 0.3 turn.1
  27.9 0.0 collective-permute-done.5.refs_1_
  27.9 0.0 collective-permute-done.6.refs_2_
  27.9 1.5 %collective-permute-start.15 = (bf16[576,128]{1,0:T(8,128)(2,1)S(1)}, bf16[576,128]{1,0:T(8,128)(2,1)S(1)}, u32[]{:S(2)}, u32[]{:S(2)}) collective-permute-start(bf16[576,128]{1,0:T(8,128)(2,1)S(1)} %join.2.refs_0_), channel_id=1, source_target_pairs={{0,2},{2,0},{4,6},{6,4},{8,10},{10,8},{12,14},{14,12},{1,3},{3,1},... | collective-permute-start | bytes 442376 | tf_op jit(solution)/shard_map/ppermute | solution.py:30
  29.5 0.0 copy-done.1
  29.5 0.5 signs.1
  29.9 0.0 collective-permute-done.11.refs_0_
  29.9 1.7 %collective-permute-done.12.refs_1_ = bf16[144,128]{1,0:T(8,128)(2,1)S(1)} collective-permute-done((bf16[144,128]{1,0:T(8,128)(2,1)S(1)}, bf16[144,128]{1,0:T(8,128)(2,1)S(1)}, u32[]{:S(2)}, u32[]{:S(2)}) %collective-permute-start.12) | collective-permute-done | bytes 36896 | tf_op jit(solution)/shard_map/ppermute | solution.py:30
  31.7 0.0 collective-permute-done.13.refs_2_
  31.7 1.3 %collective-permute-start.14 = (bf16[576,128]{1,0:T(8,128)(2,1)S(1)}, bf16[576,128]{1,0:T(8,128)(2,1)S(1)}, u32[]{:S(2)}, u32[]{:S(2)}) collective-permute-start(bf16[576,128]{1,0:T(8,128)(2,1)S(1)} %join.3.refs_0_), channel_id=1, source_target_pairs={{0,2},{2,0},{4,6},{6,4},{8,10},{10,8},{12,14},{14,12},{1,3},{3,1},... | collective-permute-start | bytes 442376 | tf_op jit(solution)/shard_map/ppermute | solution.py:30
  33.0 0.3 collective-permute-done.15.refs_1_
  33.4 0.0 copy-done
  33.4 2.0 %wide.1.refs_4_ = f32[5376,128]{1,0:T(8,128)S(1)} custom-call(bf16[576,128]{1,0:T(8,128)(2,1)S(1)} %join.2.refs_0_, bf16[576,128]{1,0:T(8,128)(2,1)S(1)} %collective-permute-done.15.refs_1_, bf16[1792,384]{1,0:T(8,128)(2,1)S(1)} %get-tuple-element.53.refs_2_, bf16[1792,384]{1,0:T(8,128)(2,1)S(1)} %get-tuple-element.54.refs_3_, ...), custom_call_target="tpu_custom_call" | custom-call | flops 1000000000 | bytes 10000000 | tf_op jit(solution)/shard_map/wide/pallas_call | solution.py:357
  35.4 1.6 %collective-permute-done.14.refs_1_ = bf16[576,128]{1,0:T(8,128)(2,1)S(1)} collective-permute-done((bf16[576,128]{1,0:T(8,128)(2,1)S(1)}, bf16[576,128]{1,0:T(8,128)(2,1)S(1)}, u32[]{:S(2)}, u32[]{:S(2)}) %collective-permute-start.14) | collective-permute-done | bytes 147488 | tf_op jit(solution)/shard_map/ppermute | solution.py:30
  36.9 1.5 %along_rows.1 = f32[8192,128]{1,0:T(8,128)S(1)} custom-call(bf16[576,128]{1,0:T(8,128)(2,1)S(1)} %join.3.refs_0_, bf16[576,128]{1,0:T(8,128)(2,1)S(1)} %collective-permute-done.14.refs_1_, bf16[512,384]{1,0:T(8,128)(2,1)S(1)} %get-tuple-element.33.refs_2_, bf16[512,384]{1,0:T(8,128)(2,1)S(1)} %get-tuple-element.34.refs_3_, f32[5376,128]{1,0:T(8,128)S(1)} %wide.1.refs_4_, ...), custom_call_target="tpu_custom_call" | custom-call | tf_op jit(solution)/shard_map/along_rows/pallas_call | solution.py:419
  38.5 7.7 %picked.1 = f32[8192,1,128]{2,1,0:T(1,128)S(1)} custom-call(f32[8192,1,128]{2,1,0:T(1,128)S(1)} %bitcast.15, s32[8192]{0:T(1024)S(1)} %and_or_fusion.where), custom_call_target="tpu_custom_call" | custom-call | tf_op jit(solution)/shard_map/picked/pallas_call | solution.py:486
  46.2 1.2 %sampled.1 = f32[1,8192]{1,0:T(1,128)S(1)} custom-call(f32[8192,128]{1,0:T(8,128)S(1)} %bitcast.18, bf16[128,8192]{1,0:T(8,128)(2,1)S(1)} %signs.1), custom_call_target="tpu_custom_call" | custom-call | tf_op jit(solution)/shard_map/sampled/pallas_call | solution.py:514
  47.4 0.1 collective-permute-start.16
  47.5 1.2 %collective-permute-done.16 = f32[1,8192]{1,0:T(1,128)S(1)} collective-permute-done((f32[1,8192]{1,0:T(1,128)S(1)}, f32[1,8192]{1,0:T(1,128)S(1)}, u32[]{:S(2)}, u32[]{:S(2)}) %collective-permute-start.16) | collective-permute-done | bytes 32800 | tf_op jit(solution)/shard_map/ppermute | solution.py:30
  48.7 1.9 %collective-permute-start.17 = (f32[1,8192]{1,0:T(1,128)S(1)}, f32[1,8192]{1,0:T(1,128)S(1)}, u32[]{:S(2)}, u32[]{:S(2)}) collective-permute-start(f32[1,8192]{1,0:T(1,128)S(1)} %add.15), channel_id=1, source_target_pairs={{1,8},{3,10},{5,12},{7,14},{9,0},{11,2},{13,4},{15,6},{0,9},{2,11}... | collective-permute-start | bytes 98312 | tf_op jit(solution)/shard_map/ppermute | solution.py:275
  50.6 1.5 %collective-permute-start.18 = (f32[1,8192]{1,0:T(1,128)S(1)}, f32[1,8192]{1,0:T(1,128)S(1)}, u32[]{:S(2)}, u32[]{:S(2)}) collective-permute-start(f32[1,8192]{1,0:T(1,128)S(1)} %add.15), channel_id=1, source_target_pairs={{1,2},{3,0},{5,6},{7,4},{9,10},{11,8},{13,14},{15,12},{0,11},{2,9}... | collective-permute-start | bytes 98312 | tf_op jit(solution)/shard_map/ppermute | solution.py:275
  52.1 0.0 collective-permute-start.19
  52.1 3.5 %collective-permute-start.20 = (f32[1,8192]{1,0:T(1,128)S(1)}, f32[1,8192]{1,0:T(1,128)S(1)}, u32[]{:S(2)}, u32[]{:S(2)}) collective-permute-start(f32[1,8192]{1,0:T(1,128)S(1)} %add.15), channel_id=1, source_target_pairs={{1,6},{3,4},{5,2},{7,0},{9,14},{11,12},{13,10},{15,8},{0,15},{2,13... | collective-permute-start | bytes 98312 | tf_op jit(solution)/shard_map/ppermute | solution.py:275
  55.6 0.0 collective-permute-done.17
  55.6 0.0 collective-permute-done.18
  55.6 0.0 collective-permute-done.19
  55.6 1.6 %collective-permute-done.20 = f32[1,8192]{1,0:T(1,128)S(1)} collective-permute-done((f32[1,8192]{1,0:T(1,128)S(1)}, f32[1,8192]{1,0:T(1,128)S(1)}, u32[]{:S(2)}, u32[]{:S(2)}) %collective-permute-start.20) | collective-permute-done | bytes 32800 | tf_op jit(solution)/shard_map/ppermute | solution.py:275
  57.2 0.1 fusion.1
  57.3 1.3 %collective-permute-start.21 = (f32[1,8192]{1,0:T(1,128)S(1)}, f32[1,8192]{1,0:T(1,128)S(1)}, u32[]{:S(2)}, u32[]{:S(2)}) collective-permute-start(f32[1,8192]{1,0:T(1,128)S(1)} %fusion.1), channel_id=1, source_target_pairs={{0,1},{1,0},{2,3},{3,2},{4,5},{5,4},{6,7},{7,6},{8,9},{9,8},{10,11... | collective-permute-start | bytes 98312 | tf_op jit(solution)/shard_map/ppermute | solution.py:30
  58.5 0.9 %collective-permute-done.21 = f32[1,8192]{1,0:T(1,128)S(1)} collective-permute-done((f32[1,8192]{1,0:T(1,128)S(1)}, f32[1,8192]{1,0:T(1,128)S(1)}, u32[]{:S(2)}, u32[]{:S(2)}) %collective-permute-start.21) | collective-permute-done | bytes 32800 | tf_op jit(solution)/shard_map/ppermute | solution.py:30
  59.4 0.6 %add.19 = f32[1,8192]{1,0:T(1,128)} add(f32[1,8192]{1,0:T(1,128)S(1)} %fusion.1, f32[1,8192]{1,0:T(1,128)S(1)} %collective-permute-done.21) | non-fusion elementwise | flops 8192 | bytes 98304 | tf_op jit(solution)/shard_map/add | solution.py:279
  (8 shorter events, 0.2 us)
Async XLA Ops:
  1.9 7.0 %collective-permute-start = (bf16[576,128]{1,0:T(8,128)(2,1)S(1)}, bf16[576,128]{1,0:T(8,128)(2,1)S(1)}, u32[]{:S(2)}, u32[]{:S(2)}) collective-permute-start(bf16[576,128]{1,0:T(8,128)(2,1)S(1)} %get-tuple-element.36), channel_id=1, source_target_pairs={{0,2},{2,0},{4,6},{6,4},{8,10},{10,8},{12,14},{14,12},{1,3},{3,1},... | collective-permute-start | bytes 442376 | tf_op jit(solution)/shard_map/ppermute | solution.py:30
  8.7 20.7 %copy-start.1 = (s32[8192]{0:T(1024)S(1)}, s32[8192]{0:T(1024)}, u32[]{:S(2)}) copy-start(s32[8192]{0:T(1024)} %param.25) | copy-start | bytes 98308
  8.8 5.4 %collective-permute-start.7 = (bf16[576,128]{1,0:T(8,128)(2,1)S(1)}, bf16[576,128]{1,0:T(8,128)(2,1)S(1)}, u32[]{:S(2)}, u32[]{:S(2)}) collective-permute-start(bf16[576,128]{1,0:T(8,128)(2,1)S(1)} %get-tuple-element.45), channel_id=1, source_target_pairs={{0,2},{2,0},{4,6},{6,4},{8,10},{10,8},{12,14},{14,12},{1,3},{3,1},... | collective-permute-start | bytes 442376 | tf_op jit(solution)/shard_map/ppermute | solution.py:30
  8.9 8.9 %collective-permute-start.1 = (bf16[144,128]{1,0:T(8,128)(2,1)S(1)}, bf16[144,128]{1,0:T(8,128)(2,1)S(1)}, u32[]{:S(2)}, u32[]{:S(2)}) collective-permute-start(bf16[144,128]{1,0:T(8,128)(2,1)S(1)} %get-tuple-element.38), channel_id=1, source_target_pairs={{0,12},{2,14},{4,8},{6,10},{8,4},{10,6},{12,0},{14,2},{1,13},{3,15... | collective-permute-start | bytes 110600 | tf_op jit(solution)/shard_map/ppermute | solution.py:30
  13.1 5.6 %collective-permute-start.2 = (bf16[144,128]{1,0:T(8,128)(2,1)S(1)}, bf16[144,128]{1,0:T(8,128)(2,1)S(1)}, u32[]{:S(2)}, u32[]{:S(2)}) collective-permute-start(bf16[144,128]{1,0:T(8,128)(2,1)S(1)} %get-tuple-element.39), channel_id=1, source_target_pairs={{0,8},{2,10},{4,12},{6,14},{8,0},{10,2},{12,4},{14,6},{1,9},{3,11}... | collective-permute-start | bytes 110600 | tf_op jit(solution)/shard_map/ppermute | solution.py:30
  13.1 5.6 %collective-permute-start.3 = (bf16[144,128]{1,0:T(8,128)(2,1)S(1)}, bf16[144,128]{1,0:T(8,128)(2,1)S(1)}, u32[]{:S(2)}, u32[]{:S(2)}) collective-permute-start(bf16[144,128]{1,0:T(8,128)(2,1)S(1)} %get-tuple-element.40), channel_id=1, source_target_pairs={{0,4},{2,6},{4,0},{6,2},{8,12},{10,14},{12,8},{14,10},{1,5},{3,7},... | collective-permute-start | bytes 110600 | tf_op jit(solution)/shard_map/ppermute | solution.py:30
  14.1 19.3 %copy-start = (s32[1048576]{0:T(1024)S(1)}, s32[1048576]{0:T(1024)}, u32[]{:S(2)}) copy-start(s32[1048576]{0:T(1024)} %param.24) | copy-start | bytes 12582916
  14.2 8.2 %collective-permute-start.10 = (bf16[144,128]{1,0:T(8,128)(2,1)S(1)}, bf16[144,128]{1,0:T(8,128)(2,1)S(1)}, u32[]{:S(2)}, u32[]{:S(2)}) collective-permute-start(bf16[144,128]{1,0:T(8,128)(2,1)S(1)} %get-tuple-element.50), channel_id=1, source_target_pairs={{0,12},{2,14},{4,8},{6,10},{8,4},{10,6},{12,0},{14,2},{1,13},{3,15... | collective-permute-start | bytes 110600 | tf_op jit(solution)/shard_map/ppermute | solution.py:30
  17.8 5.3 %collective-permute-start.8 = (bf16[144,128]{1,0:T(8,128)(2,1)S(1)}, bf16[144,128]{1,0:T(8,128)(2,1)S(1)}, u32[]{:S(2)}, u32[]{:S(2)}) collective-permute-start(bf16[144,128]{1,0:T(8,128)(2,1)S(1)} %get-tuple-element.48), channel_id=1, source_target_pairs={{0,8},{2,10},{4,12},{6,14},{8,0},{10,2},{12,4},{14,6},{1,9},{3,11}... | collective-permute-start | bytes 110600 | tf_op jit(solution)/shard_map/ppermute | solution.py:30
  17.9 5.3 %collective-permute-start.9 = (bf16[144,128]{1,0:T(8,128)(2,1)S(1)}, bf16[144,128]{1,0:T(8,128)(2,1)S(1)}, u32[]{:S(2)}, u32[]{:S(2)}) collective-permute-start(bf16[144,128]{1,0:T(8,128)(2,1)S(1)} %get-tuple-element.49), channel_id=1, source_target_pairs={{0,4},{2,6},{4,0},{6,2},{8,12},{10,14},{12,8},{14,10},{1,5},{3,7},... | collective-permute-start | bytes 110600 | tf_op jit(solution)/shard_map/ppermute | solution.py:30
  18.7 8.2 %collective-permute-start.4 = (bf16[144,128]{1,0:T(8,128)(2,1)S(1)}, bf16[144,128]{1,0:T(8,128)(2,1)S(1)}, u32[]{:S(2)}, u32[]{:S(2)}) collective-permute-start(bf16[144,128]{1,0:T(8,128)(2,1)S(1)} %add_up.5.own), channel_id=1, source_target_pairs={{0,12},{2,14},{4,8},{6,10},{8,4},{10,6},{12,0},{14,2},{1,13},{3,15... | collective-permute-start | bytes 110600 | tf_op jit(solution)/shard_map/ppermute | solution.py:30
  22.3 5.5 %collective-permute-start.5 = (bf16[144,128]{1,0:T(8,128)(2,1)S(1)}, bf16[144,128]{1,0:T(8,128)(2,1)S(1)}, u32[]{:S(2)}, u32[]{:S(2)}) collective-permute-start(bf16[144,128]{1,0:T(8,128)(2,1)S(1)} %add_up.5.own), channel_id=1, source_target_pairs={{0,8},{2,10},{4,12},{6,14},{8,0},{10,2},{12,4},{14,6},{1,9},{3,11}... | collective-permute-start | bytes 110600 | tf_op jit(solution)/shard_map/ppermute | solution.py:30
  22.3 5.5 %collective-permute-start.6 = (bf16[144,128]{1,0:T(8,128)(2,1)S(1)}, bf16[144,128]{1,0:T(8,128)(2,1)S(1)}, u32[]{:S(2)}, u32[]{:S(2)}) collective-permute-start(bf16[144,128]{1,0:T(8,128)(2,1)S(1)} %add_up.5.own), channel_id=1, source_target_pairs={{0,4},{2,6},{4,0},{6,2},{8,12},{10,14},{12,8},{14,10},{1,5},{3,7},... | collective-permute-start | bytes 110600 | tf_op jit(solution)/shard_map/ppermute | solution.py:30
  23.2 6.8 %collective-permute-start.11 = (bf16[144,128]{1,0:T(8,128)(2,1)S(1)}, bf16[144,128]{1,0:T(8,128)(2,1)S(1)}, u32[]{:S(2)}, u32[]{:S(2)}) collective-permute-start(bf16[144,128]{1,0:T(8,128)(2,1)S(1)} %add_up.7.own), channel_id=1, source_target_pairs={{0,12},{2,14},{4,8},{6,10},{8,4},{10,6},{12,0},{14,2},{1,13},{3,15... | collective-permute-start | bytes 110600 | tf_op jit(solution)/shard_map/ppermute | solution.py:30
  26.8 4.9 %collective-permute-start.12 = (bf16[144,128]{1,0:T(8,128)(2,1)S(1)}, bf16[144,128]{1,0:T(8,128)(2,1)S(1)}, u32[]{:S(2)}, u32[]{:S(2)}) collective-permute-start(bf16[144,128]{1,0:T(8,128)(2,1)S(1)} %add_up.7.own), channel_id=1, source_target_pairs={{0,8},{2,10},{4,12},{6,14},{8,0},{10,2},{12,4},{14,6},{1,9},{3,11}... | collective-permute-start | bytes 110600 | tf_op jit(solution)/shard_map/ppermute | solution.py:30
  26.8 4.9 %collective-permute-start.13 = (bf16[144,128]{1,0:T(8,128)(2,1)S(1)}, bf16[144,128]{1,0:T(8,128)(2,1)S(1)}, u32[]{:S(2)}, u32[]{:S(2)}) collective-permute-start(bf16[144,128]{1,0:T(8,128)(2,1)S(1)} %add_up.7.own), channel_id=1, source_target_pairs={{0,4},{2,6},{4,0},{6,2},{8,12},{10,14},{12,8},{14,10},{1,5},{3,7},... | collective-permute-start | bytes 110600 | tf_op jit(solution)/shard_map/ppermute | solution.py:30
  27.9 5.4 %collective-permute-start.15 = (bf16[576,128]{1,0:T(8,128)(2,1)S(1)}, bf16[576,128]{1,0:T(8,128)(2,1)S(1)}, u32[]{:S(2)}, u32[]{:S(2)}) collective-permute-start(bf16[576,128]{1,0:T(8,128)(2,1)S(1)} %join.2.refs_0_), channel_id=1, source_target_pairs={{0,2},{2,0},{4,6},{6,4},{8,10},{10,8},{12,14},{14,12},{1,3},{3,1},... | collective-permute-start | bytes 442376 | tf_op jit(solution)/shard_map/ppermute | solution.py:30
  31.7 5.2 %collective-permute-start.14 = (bf16[576,128]{1,0:T(8,128)(2,1)S(1)}, bf16[576,128]{1,0:T(8,128)(2,1)S(1)}, u32[]{:S(2)}, u32[]{:S(2)}) collective-permute-start(bf16[576,128]{1,0:T(8,128)(2,1)S(1)} %join.3.refs_0_), channel_id=1, source_target_pairs={{0,2},{2,0},{4,6},{6,4},{8,10},{10,8},{12,14},{14,12},{1,3},{3,1},... | collective-permute-start | bytes 442376 | tf_op jit(solution)/shard_map/ppermute | solution.py:30
  47.4 1.3 %collective-permute-start.16 = (f32[1,8192]{1,0:T(1,128)S(1)}, f32[1,8192]{1,0:T(1,128)S(1)}, u32[]{:S(2)}, u32[]{:S(2)}) collective-permute-start(f32[1,8192]{1,0:T(1,128)S(1)} %sampled.1), channel_id=1, source_target_pairs={{0,1},{1,0},{2,3},{3,2},{4,5},{5,4},{6,7},{7,6},{8,9},{9,8},{10,11... | collective-permute-start | bytes 98312 | tf_op jit(solution)/shard_map/ppermute | solution.py:30
  48.7 6.9 %collective-permute-start.17 = (f32[1,8192]{1,0:T(1,128)S(1)}, f32[1,8192]{1,0:T(1,128)S(1)}, u32[]{:S(2)}, u32[]{:S(2)}) collective-permute-start(f32[1,8192]{1,0:T(1,128)S(1)} %add.15), channel_id=1, source_target_pairs={{1,8},{3,10},{5,12},{7,14},{9,0},{11,2},{13,4},{15,6},{0,9},{2,11}... | collective-permute-start | bytes 98312 | tf_op jit(solution)/shard_map/ppermute | solution.py:275
  50.6 5.0 %collective-permute-start.18 = (f32[1,8192]{1,0:T(1,128)S(1)}, f32[1,8192]{1,0:T(1,128)S(1)}, u32[]{:S(2)}, u32[]{:S(2)}) collective-permute-start(f32[1,8192]{1,0:T(1,128)S(1)} %add.15), channel_id=1, source_target_pairs={{1,2},{3,0},{5,6},{7,4},{9,10},{11,8},{13,14},{15,12},{0,11},{2,9}... | collective-permute-start | bytes 98312 | tf_op jit(solution)/shard_map/ppermute | solution.py:275
  52.1 3.5 %collective-permute-start.19 = (f32[1,8192]{1,0:T(1,128)S(1)}, f32[1,8192]{1,0:T(1,128)S(1)}, u32[]{:S(2)}, u32[]{:S(2)}) collective-permute-start(f32[1,8192]{1,0:T(1,128)S(1)} %add.15), channel_id=1, source_target_pairs={{1,4},{3,6},{5,0},{7,2},{9,12},{11,14},{13,8},{15,10},{0,13},{2,15... | collective-permute-start | bytes 98312 | tf_op jit(solution)/shard_map/ppermute | solution.py:275
  52.1 5.1 %collective-permute-start.20 = (f32[1,8192]{1,0:T(1,128)S(1)}, f32[1,8192]{1,0:T(1,128)S(1)}, u32[]{:S(2)}, u32[]{:S(2)}) collective-permute-start(f32[1,8192]{1,0:T(1,128)S(1)} %add.15), channel_id=1, source_target_pairs={{1,6},{3,4},{5,2},{7,0},{9,14},{11,12},{13,10},{15,8},{0,15},{2,13... | collective-permute-start | bytes 98312 | tf_op jit(solution)/shard_map/ppermute | solution.py:275
  57.3 2.1 %collective-permute-start.21 = (f32[1,8192]{1,0:T(1,128)S(1)}, f32[1,8192]{1,0:T(1,128)S(1)}, u32[]{:S(2)}, u32[]{:S(2)}) collective-permute-start(f32[1,8192]{1,0:T(1,128)S(1)} %fusion.1), channel_id=1, source_target_pairs={{0,1},{1,0},{2,3},{3,2},{4,5},{5,4},{6,7},{7,6},{8,9},{9,8},{10,11... | collective-permute-start | bytes 98312 | tf_op jit(solution)/shard_map/ppermute | solution.py:30
where the time goes:
time: 60.2 us; the launch traced here: 60 us
  starting transfers between devices  32.3 us (54%)
  Pallas kernels  19 us (32%)
  waiting for transfers between devices  7.77 us (13%)
  other arithmetic  0.77 us (1%)
    ppermute x18, starting transfers between devices, exchange(): return lax.ppermute(value, axis, pairs)  25.4 us
    pallas_call x1, Pallas kernels, picked(): pl.pallas_call(pick_kernel, out_shape=jax.ShapeDtypeStruct((samples, 1, r...  7.68 us
    ppermute x4, starting transfers between devices, total_over(): got = lax.ppermute(total, ('coord', 'ckpt'), pairs)  6.85 us
    ppermute x18, waiting for transfers between devices, exchange(): return lax.ppermute(value, axis, pairs)  6.18 us
    pallas_call x1, Pallas kernels, long_products(): pl.pallas_call(functools.partial(long_kernel, stage, cut), out_shape=shap...  3.76 us
    pallas_call x1, Pallas kernels, wide(): pl.pallas_call(functools.partial(wide_kernel, aligned, block, first, stag...  1.98 us
    pallas_call x1, Pallas kernels, short_products(): pl.pallas_call(functools.partial(short_kernel, stage, cuts), out_shape=sh...  1.9 us
    ppermute x4, waiting for transfers between devices, total_over(): got = lax.ppermute(total, ('coord', 'ckpt'), pairs)  1.59 us
  transfers between devices with their start and end apart: 22, of which 7 were waited for; matrix products, arithmetic and copies ran while one was open for 0% of the time, Pallas kernels for 11%

commit v1 on v0

--- a/solution.py
+++ b/solution.py
@@ -404,14 +404,9 @@
             return None
         return wide_mix[pl.ds(i * block - first + begin, 8), :]
 
-    def across(step, _):
-        begin = pl.multiple_of(step * 8, 8)
+    for begin in range(0, block, 8):
         for i, value in enumerate(butterflies([load(i, begin) for i in range(number)])):
-            mix[pl.ds(i * block + begin, 8), :] = value
-        return _
-
-    if number > 1:
-        lax.fori_loop(0, block // 8, across, 0, unroll=4)
+            mix[i * block + begin : i * block + begin + 8, :] = value
 
 
 def along_rows(aligned, block, stage, length, parts, x_t, go_t, wide_mix, flags):
@@ -464,34 +459,40 @@
 
 
 def pick_kernel(mix, where, rows):
-    samples = rows.shape[0]
-    unroll, ahead = min(256, samples), 16
+    samples, rank = rows.shape
+    group = min(128, samples)
+    unroll = min(2, samples // group)
+    place = lax.broadcasted_iota(jnp.int32, (8, rank), 0)
+    masks = [place == i for i in range(8)]
+
+    def picked_tile(sources, begin):
+        tile = None
+        for i in range(8):
+            row = jnp.broadcast_to(mix[pl.ds(sources[begin + i], 1), :], (8, rank))
+            tile = row if tile is None else jnp.where(masks[i], row, tile)
+        return tile
 
     def pick(step, _):
-        begin = step * unroll
-        held = []
-        for i in range(unroll):
-            held.append(mix[where[begin + i]])
-            if i >= ahead:
-                rows[begin + i - ahead] = held[i - ahead]
-        for i in range(unroll - ahead, unroll):
-            rows[begin + i] = held[i]
+        for part in range(unroll):
+            span = pl.ds(pl.multiple_of((step * unroll + part) * group, group), group)
+            sources, targets = where.at[span], rows.at[span]
+            tiles = [picked_tile(sources, begin) for begin in range(0, group, 8)]
+            for i, tile in enumerate(tiles):
+                targets[8 * i : 8 * i + 8, :] = tile
         return _
 
-    lax.fori_loop(0, samples // unroll, pick, 0)
+    lax.fori_loop(0, samples // (group * unroll), pick, 0)
 
 
 def picked(mix, where):
-    rank, samples = mix.shape[1], where.shape[0]
-    rows = pl.pallas_call(
+    return pl.pallas_call(
         pick_kernel,
-        out_shape=jax.ShapeDtypeStruct((samples, 1, rank), F32),
+        out_shape=jax.ShapeDtypeStruct((where.shape[0], mix.shape[1]), F32),
         in_specs=[VMEM, SMEM],
         out_specs=VMEM,
         compiler_params=limit(4),
         name="picked",
-    )(mix.reshape(-1, 1, rank), where)
-    return rows.reshape(samples, rank)
+    )(mix, where)
 
 
 def sample_kernel(final_scale, rows, signs, out):

time: 60.2 us -> 60.1 us (level)
  no operation moved by 1% of the time
where the time goes in v1:
time: 60.1 us; the launch traced here: 60 us
  starting transfers between devices  32.3 us (54%)
  Pallas kernels  19 us (32%)
  waiting for transfers between devices  7.77 us (13%)
  other arithmetic  0.77 us (1%)
    ppermute x18, starting transfers between devices, exchange(): return lax.ppermute(value, axis, pairs)  25.5 us
    pallas_call x1, Pallas kernels, picked(): pl.pallas_call(pick_kernel, out_shape=jax.ShapeDtypeStruct((where.shape[0...  7.63 us
    ppermute x4, starting transfers between devices, total_over(): got = lax.ppermute(total, ('coord', 'ckpt'), pairs)  6.82 us
    ppermute x18, waiting for transfers between devices, exchange(): return lax.ppermute(value, axis, pairs)  6.18 us
    pallas_call x1, Pallas kernels, long_products(): pl.pallas_call(functools.partial(long_kernel, stage, cut), out_shape=shap...  3.76 us
    pallas_call x1, Pallas kernels, wide(): pl.pallas_call(functools.partial(wide_kernel, aligned, block, first, stag...  1.98 us
    pallas_call x1, Pallas kernels, short_products(): pl.pallas_call(functools.partial(short_kernel, stage, cuts), out_shape=sh...  1.9 us
    ppermute x4, waiting for transfers between devices, total_over(): got = lax.ppermute(total, ('coord', 'ckpt'), pairs)  1.59 us
  transfers between devices with their start and end apart: 22, of which 7 were waited for; matrix products, arithmetic and copies ran while one was open for 0% of the time, Pallas kernels for 11%

profile of v1, /device:TPU:0, one launch (start us, length us, event | category | flops | bytes accessed | tf_op | source)
XLA Modules:
  0.0 60.0 jit_solution(4767716907221333950)
XLA Ops:
  0.0 1.9 %short.1 = (bf16[384,512]{1,0:T(8,128)(2,1)S(1)}, bf16[384,512]{1,0:T(8,128)(2,1)S(1)}, f32[576,128]{1,0:T(8,128)S(1)}, bf16[576,128]{1,0:T(8,128)(2,1)S(1)}) custom-call(bf16[384,512]{1,0:T(8,128)(2,1)} %bitcast.22, bf16[384,512]{1,0:T(8,128)(2,1)} %bitcast.23, bf16[512,128]{1,0:T(8,128)(2,1)} %bitcast.24, bf16[512,128]{1,0:T(8,128)(2,1)} %bitcast.25, ...), custom_call_target="tpu_custom_call" | custom-call | flops 100000000 | bytes 6000000 | tf_op jit(solution)/shard_map/short/pallas_call | solution.py:123
  1.9 3.1 %collective-permute-start = (bf16[576,128]{1,0:T(8,128)(2,1)S(1)}, bf16[576,128]{1,0:T(8,128)(2,1)S(1)}, u32[]{:S(2)}, u32[]{:S(2)}) collective-permute-start(bf16[576,128]{1,0:T(8,128)(2,1)S(1)} %get-tuple-element.36), channel_id=1, source_target_pairs={{0,2},{2,0},{4,6},{6,4},{8,10},{10,8},{12,14},{14,12},{1,3},{3,1},... | collective-permute-start | bytes 442376 | tf_op jit(solution)/shard_map/ppermute | solution.py:30
  5.0 3.8 %long.1 = (bf16[1792,384]{1,0:T(8,128)(2,1)S(1)}, bf16[1792,384]{1,0:T(8,128)(2,1)S(1)}, bf16[1792,384]{1,0:T(8,128)(2,1)S(1)}, f32[576,128]{1,0:T(8,128)S(1)}, bf16[576,128]{1,0:T(8,128)(2,1)S(1)}) custom-call(bf16[1792,384]{1,0:T(8,128)(2,1)} %bitcast.16, bf16[1792,384]{1,0:T(8,128)(2,1)} %bitcast.17, bf16[1792,384]{1,0:T(8,128)(2,1)} %bitcast.18, ...), custom_call_target="tpu_custom_call" | custom-call | flops 1000000000 | bytes 8000000 | tf_op jit(solution)/shard_map/long/pallas_call | solution.py:174
  8.7 0.0 copy-start.1
  8.8 0.1 collective-permute-start.7
  8.9 0.0 collective-permute-done.refs_1_
  8.9 4.1 %collective-permute-start.1 = (bf16[144,128]{1,0:T(8,128)(2,1)S(1)}, bf16[144,128]{1,0:T(8,128)(2,1)S(1)}, u32[]{:S(2)}, u32[]{:S(2)}) collective-permute-start(bf16[144,128]{1,0:T(8,128)(2,1)S(1)} %get-tuple-element.38), channel_id=1, source_target_pairs={{0,12},{2,14},{4,8},{6,10},{8,4},{10,6},{12,0},{14,2},{1,13},{3,15... | collective-permute-start | bytes 110600 | tf_op jit(solution)/shard_map/ppermute | solution.py:30
  13.1 0.0 collective-permute-start.2
  13.1 0.6 %collective-permute-start.3 = (bf16[144,128]{1,0:T(8,128)(2,1)S(1)}, bf16[144,128]{1,0:T(8,128)(2,1)S(1)}, u32[]{:S(2)}, u32[]{:S(2)}) collective-permute-start(bf16[144,128]{1,0:T(8,128)(2,1)S(1)} %get-tuple-element.40), channel_id=1, source_target_pairs={{0,4},{2,6},{4,0},{6,2},{8,12},{10,14},{12,8},{14,10},{1,5},{3,7},... | collective-permute-start | bytes 110600 | tf_op jit(solution)/shard_map/ppermute | solution.py:30
  13.7 0.4 collective-permute-done.7.refs_1_
  14.1 0.0 copy-start
  14.2 3.7 %collective-permute-start.10 = (bf16[144,128]{1,0:T(8,128)(2,1)S(1)}, bf16[144,128]{1,0:T(8,128)(2,1)S(1)}, u32[]{:S(2)}, u32[]{:S(2)}) collective-permute-start(bf16[144,128]{1,0:T(8,128)(2,1)S(1)} %get-tuple-element.50), channel_id=1, source_target_pairs={{0,12},{2,14},{4,8},{6,10},{8,4},{10,6},{12,0},{14,2},{1,13},{3,15... | collective-permute-start | bytes 110600 | tf_op jit(solution)/shard_map/ppermute | solution.py:30
  17.8 0.0 collective-permute-start.8
  17.8 0.0 collective-permute-done.1.refs_1_
  17.9 0.8 %collective-permute-start.9 = (bf16[144,128]{1,0:T(8,128)(2,1)S(1)}, bf16[144,128]{1,0:T(8,128)(2,1)S(1)}, u32[]{:S(2)}, u32[]{:S(2)}) collective-permute-start(bf16[144,128]{1,0:T(8,128)(2,1)S(1)} %get-tuple-element.49), channel_id=1, source_target_pairs={{0,4},{2,6},{4,0},{6,2},{8,12},{10,14},{12,8},{14,10},{1,5},{3,7},... | collective-permute-start | bytes 110600 | tf_op jit(solution)/shard_map/ppermute | solution.py:30
  18.6 0.0 collective-permute-done.2.refs_2_
  18.6 0.0 collective-permute-done.3.refs_3_
  18.7 3.7 %collective-permute-start.4 = (bf16[144,128]{1,0:T(8,128)(2,1)S(1)}, bf16[144,128]{1,0:T(8,128)(2,1)S(1)}, u32[]{:S(2)}, u32[]{:S(2)}) collective-permute-start(bf16[144,128]{1,0:T(8,128)(2,1)S(1)} %add_up.5.own), channel_id=1, source_target_pairs={{0,12},{2,14},{4,8},{6,10},{8,4},{10,6},{12,0},{14,2},{1,13},{3,15... | collective-permute-start | bytes 110600 | tf_op jit(solution)/shard_map/ppermute | solution.py:30
  22.3 0.0 collective-permute-start.5
  22.3 0.0 collective-permute-done.10.refs_3_
  22.3 0.8 %collective-permute-start.6 = (bf16[144,128]{1,0:T(8,128)(2,1)S(1)}, bf16[144,128]{1,0:T(8,128)(2,1)S(1)}, u32[]{:S(2)}, u32[]{:S(2)}) collective-permute-start(bf16[144,128]{1,0:T(8,128)(2,1)S(1)} %add_up.5.own), channel_id=1, source_target_pairs={{0,4},{2,6},{4,0},{6,2},{8,12},{10,14},{12,8},{14,10},{1,5},{3,7},... | collective-permute-start | bytes 110600 | tf_op jit(solution)/shard_map/ppermute | solution.py:30
  23.1 0.0 collective-permute-done.8.refs_1_
  23.1 0.0 collective-permute-done.9.refs_2_
  23.2 3.7 %collective-permute-start.11 = (bf16[144,128]{1,0:T(8,128)(2,1)S(1)}, bf16[144,128]{1,0:T(8,128)(2,1)S(1)}, u32[]{:S(2)}, u32[]{:S(2)}) collective-permute-start(bf16[144,128]{1,0:T(8,128)(2,1)S(1)} %add_up.7.own), channel_id=1, source_target_pairs={{0,12},{2,14},{4,8},{6,10},{8,4},{10,6},{12,0},{14,2},{1,13},{3,15... | collective-permute-start | bytes 110600 | tf_op jit(solution)/shard_map/ppermute | solution.py:30
  26.8 0.0 collective-permute-start.12
  26.8 0.0 collective-permute-done.4.refs_0_
  26.8 0.8 %collective-permute-start.13 = (bf16[144,128]{1,0:T(8,128)(2,1)S(1)}, bf16[144,128]{1,0:T(8,128)(2,1)S(1)}, u32[]{:S(2)}, u32[]{:S(2)}) collective-permute-start(bf16[144,128]{1,0:T(8,128)(2,1)S(1)} %add_up.7.own), channel_id=1, source_target_pairs={{0,4},{2,6},{4,0},{6,2},{8,12},{10,14},{12,8},{14,10},{1,5},{3,7},... | collective-permute-start | bytes 110600 | tf_op jit(solution)/shard_map/ppermute | solution.py:30
  27.6 0.3 turn.1
  27.9 0.0 collective-permute-done.5.refs_1_
  27.9 0.0 collective-permute-done.6.refs_2_
  27.9 1.5 %collective-permute-start.15 = (bf16[576,128]{1,0:T(8,128)(2,1)S(1)}, bf16[576,128]{1,0:T(8,128)(2,1)S(1)}, u32[]{:S(2)}, u32[]{:S(2)}) collective-permute-start(bf16[576,128]{1,0:T(8,128)(2,1)S(1)} %join.2.refs_0_), channel_id=1, source_target_pairs={{0,2},{2,0},{4,6},{6,4},{8,10},{10,8},{12,14},{14,12},{1,3},{3,1},... | collective-permute-start | bytes 442376 | tf_op jit(solution)/shard_map/ppermute | solution.py:30
  29.5 0.0 copy-done.1
  29.5 0.5 signs.1
  29.9 0.0 collective-permute-done.11.refs_0_
  29.9 1.7 %collective-permute-done.12.refs_1_ = bf16[144,128]{1,0:T(8,128)(2,1)S(1)} collective-permute-done((bf16[144,128]{1,0:T(8,128)(2,1)S(1)}, bf16[144,128]{1,0:T(8,128)(2,1)S(1)}, u32[]{:S(2)}, u32[]{:S(2)}) %collective-permute-start.12) | collective-permute-done | bytes 36896 | tf_op jit(solution)/shard_map/ppermute | solution.py:30
  31.7 0.0 collective-permute-done.13.refs_2_
  31.7 1.3 %collective-permute-start.14 = (bf16[576,128]{1,0:T(8,128)(2,1)S(1)}, bf16[576,128]{1,0:T(8,128)(2,1)S(1)}, u32[]{:S(2)}, u32[]{:S(2)}) collective-permute-start(bf16[576,128]{1,0:T(8,128)(2,1)S(1)} %join.3.refs_0_), channel_id=1, source_target_pairs={{0,2},{2,0},{4,6},{6,4},{8,10},{10,8},{12,14},{14,12},{1,3},{3,1},... | collective-permute-start | bytes 442376 | tf_op jit(solution)/shard_map/ppermute | solution.py:30
  33.0 0.3 collective-permute-done.15.refs_1_
  33.4 0.0 copy-done
  33.4 2.0 %wide.1.refs_4_ = f32[5376,128]{1,0:T(8,128)S(1)} custom-call(bf16[576,128]{1,0:T(8,128)(2,1)S(1)} %join.2.refs_0_, bf16[576,128]{1,0:T(8,128)(2,1)S(1)} %collective-permute-done.15.refs_1_, bf16[1792,384]{1,0:T(8,128)(2,1)S(1)} %get-tuple-element.53.refs_2_, bf16[1792,384]{1,0:T(8,128)(2,1)S(1)} %get-tuple-element.54.refs_3_, ...), custom_call_target="tpu_custom_call" | custom-call | flops 1000000000 | bytes 10000000 | tf_op jit(solution)/shard_map/wide/pallas_call | solution.py:357
  35.4 1.6 %collective-permute-done.14.refs_1_ = bf16[576,128]{1,0:T(8,128)(2,1)S(1)} collective-permute-done((bf16[576,128]{1,0:T(8,128)(2,1)S(1)}, bf16[576,128]{1,0:T(8,128)(2,1)S(1)}, u32[]{:S(2)}, u32[]{:S(2)}) %collective-permute-start.14) | collective-permute-done | bytes 147488 | tf_op jit(solution)/shard_map/ppermute | solution.py:30
  36.9 1.5 %along_rows.1.mix = f32[8192,128]{1,0:T(8,128)S(1)} custom-call(bf16[576,128]{1,0:T(8,128)(2,1)S(1)} %join.3.refs_0_, bf16[576,128]{1,0:T(8,128)(2,1)S(1)} %collective-permute-done.14.refs_1_, bf16[512,384]{1,0:T(8,128)(2,1)S(1)} %get-tuple-element.33.refs_2_, bf16[512,384]{1,0:T(8,128)(2,1)S(1)} %get-tuple-element.34.refs_3_, f32[5376,128]{1,0:T(8,128)S(1)} %wide.1.refs_4_, ...), custom_call_target="tpu_custom_call" | custom-call | tf_op jit(solution)/shard_map/along_rows/pallas_call | solution.py:414
  38.5 7.6 %picked.1.rows = f32[8192,128]{1,0:T(8,128)S(1)} custom-call(f32[8192,128]{1,0:T(8,128)S(1)} %along_rows.1.mix, s32[8192]{0:T(1024)S(1)} %and_or_fusion.where), custom_call_target="tpu_custom_call" | custom-call | tf_op jit(solution)/shard_map/picked/pallas_call | solution.py:488
  46.1 1.3 %sampled.1 = f32[1,8192]{1,0:T(1,128)S(1)} custom-call(f32[8192,128]{1,0:T(8,128)S(1)} %picked.1.rows, bf16[128,8192]{1,0:T(8,128)(2,1)S(1)} %signs.1), custom_call_target="tpu_custom_call" | custom-call | tf_op jit(solution)/shard_map/sampled/pallas_call | solution.py:515
  47.4 0.1 collective-permute-start.16
  47.4 1.2 %collective-permute-done.16 = f32[1,8192]{1,0:T(1,128)S(1)} collective-permute-done((f32[1,8192]{1,0:T(1,128)S(1)}, f32[1,8192]{1,0:T(1,128)S(1)}, u32[]{:S(2)}, u32[]{:S(2)}) %collective-permute-start.16) | collective-permute-done | bytes 32800 | tf_op jit(solution)/shard_map/ppermute | solution.py:30
  48.7 1.9 %collective-permute-start.17 = (f32[1,8192]{1,0:T(1,128)S(1)}, f32[1,8192]{1,0:T(1,128)S(1)}, u32[]{:S(2)}, u32[]{:S(2)}) collective-permute-start(f32[1,8192]{1,0:T(1,128)S(1)} %add.15), channel_id=1, source_target_pairs={{1,8},{3,10},{5,12},{7,14},{9,0},{11,2},{13,4},{15,6},{0,9},{2,11}... | collective-permute-start | bytes 98312 | tf_op jit(solution)/shard_map/ppermute | solution.py:275
  50.5 1.5 %collective-permute-start.18 = (f32[1,8192]{1,0:T(1,128)S(1)}, f32[1,8192]{1,0:T(1,128)S(1)}, u32[]{:S(2)}, u32[]{:S(2)}) collective-permute-start(f32[1,8192]{1,0:T(1,128)S(1)} %add.15), channel_id=1, source_target_pairs={{1,2},{3,0},{5,6},{7,4},{9,10},{11,8},{13,14},{15,12},{0,11},{2,9}... | collective-permute-start | bytes 98312 | tf_op jit(solution)/shard_map/ppermute | solution.py:275
  52.1 0.0 collective-permute-start.19
  52.1 3.4 %collective-permute-start.20 = (f32[1,8192]{1,0:T(1,128)S(1)}, f32[1,8192]{1,0:T(1,128)S(1)}, u32[]{:S(2)}, u32[]{:S(2)}) collective-permute-start(f32[1,8192]{1,0:T(1,128)S(1)} %add.15), channel_id=1, source_target_pairs={{1,6},{3,4},{5,2},{7,0},{9,14},{11,12},{13,10},{15,8},{0,15},{2,13... | collective-permute-start | bytes 98312 | tf_op jit(solution)/shard_map/ppermute | solution.py:275
  55.5 0.0 collective-permute-done.17
  55.5 0.0 collective-permute-done.18
  55.5 0.0 collective-permute-done.19
  55.5 1.6 %collective-permute-done.20 = f32[1,8192]{1,0:T(1,128)S(1)} collective-permute-done((f32[1,8192]{1,0:T(1,128)S(1)}, f32[1,8192]{1,0:T(1,128)S(1)}, u32[]{:S(2)}, u32[]{:S(2)}) %collective-permute-start.20) | collective-permute-done | bytes 32800 | tf_op jit(solution)/shard_map/ppermute | solution.py:275
  57.1 0.1 fusion.1
  57.2 1.3 %collective-permute-start.21 = (f32[1,8192]{1,0:T(1,128)S(1)}, f32[1,8192]{1,0:T(1,128)S(1)}, u32[]{:S(2)}, u32[]{:S(2)}) collective-permute-start(f32[1,8192]{1,0:T(1,128)S(1)} %fusion.1), channel_id=1, source_target_pairs={{0,1},{1,0},{2,3},{3,2},{4,5},{5,4},{6,7},{7,6},{8,9},{9,8},{10,11... | collective-permute-start | bytes 98312 | tf_op jit(solution)/shard_map/ppermute | solution.py:30
  58.5 0.9 %collective-permute-done.21 = f32[1,8192]{1,0:T(1,128)S(1)} collective-permute-done((f32[1,8192]{1,0:T(1,128)S(1)}, f32[1,8192]{1,0:T(1,128)S(1)}, u32[]{:S(2)}, u32[]{:S(2)}) %collective-permute-start.21) | collective-permute-done | bytes 32800 | tf_op jit(solution)/shard_map/ppermute | solution.py:30
  59.3 0.6 %add.19 = f32[1,8192]{1,0:T(1,128)} add(f32[1,8192]{1,0:T(1,128)S(1)} %fusion.1, f32[1,8192]{1,0:T(1,128)S(1)} %collective-permute-done.21) | non-fusion elementwise | flops 8192 | bytes 98304 | tf_op jit(solution)/shard_map/add | solution.py:279
  (8 shorter events, 0.2 us)
Async XLA Ops:
  1.9 7.0 %collective-permute-start = (bf16[576,128]{1,0:T(8,128)(2,1)S(1)}, bf16[576,128]{1,0:T(8,128)(2,1)S(1)}, u32[]{:S(2)}, u32[]{:S(2)}) collective-permute-start(bf16[576,128]{1,0:T(8,128)(2,1)S(1)} %get-tuple-element.36), channel_id=1, source_target_pairs={{0,2},{2,0},{4,6},{6,4},{8,10},{10,8},{12,14},{14,12},{1,3},{3,1},... | collective-permute-start | bytes 442376 | tf_op jit(solution)/shard_map/ppermute | solution.py:30
  8.7 20.7 %copy-start.1 = (s32[8192]{0:T(1024)S(1)}, s32[8192]{0:T(1024)}, u32[]{:S(2)}) copy-start(s32[8192]{0:T(1024)} %param.25) | copy-start | bytes 98308
  8.8 5.4 %collective-permute-start.7 = (bf16[576,128]{1,0:T(8,128)(2,1)S(1)}, bf16[576,128]{1,0:T(8,128)(2,1)S(1)}, u32[]{:S(2)}, u32[]{:S(2)}) collective-permute-start(bf16[576,128]{1,0:T(8,128)(2,1)S(1)} %get-tuple-element.45), channel_id=1, source_target_pairs={{0,2},{2,0},{4,6},{6,4},{8,10},{10,8},{12,14},{14,12},{1,3},{3,1},... | collective-permute-start | bytes 442376 | tf_op jit(solution)/shard_map/ppermute | solution.py:30
  8.9 8.9 %collective-permute-start.1 = (bf16[144,128]{1,0:T(8,128)(2,1)S(1)}, bf16[144,128]{1,0:T(8,128)(2,1)S(1)}, u32[]{:S(2)}, u32[]{:S(2)}) collective-permute-start(bf16[144,128]{1,0:T(8,128)(2,1)S(1)} %get-tuple-element.38), channel_id=1, source_target_pairs={{0,12},{2,14},{4,8},{6,10},{8,4},{10,6},{12,0},{14,2},{1,13},{3,15... | collective-permute-start | bytes 110600 | tf_op jit(solution)/shard_map/ppermute | solution.py:30
  13.1 5.6 %collective-permute-start.2 = (bf16[144,128]{1,0:T(8,128)(2,1)S(1)}, bf16[144,128]{1,0:T(8,128)(2,1)S(1)}, u32[]{:S(2)}, u32[]{:S(2)}) collective-permute-start(bf16[144,128]{1,0:T(8,128)(2,1)S(1)} %get-tuple-element.39), channel_id=1, source_target_pairs={{0,8},{2,10},{4,12},{6,14},{8,0},{10,2},{12,4},{14,6},{1,9},{3,11}... | collective-permute-start | bytes 110600 | tf_op jit(solution)/shard_map/ppermute | solution.py:30
  13.1 5.6 %collective-permute-start.3 = (bf16[144,128]{1,0:T(8,128)(2,1)S(1)}, bf16[144,128]{1,0:T(8,128)(2,1)S(1)}, u32[]{:S(2)}, u32[]{:S(2)}) collective-permute-start(bf16[144,128]{1,0:T(8,128)(2,1)S(1)} %get-tuple-element.40), channel_id=1, source_target_pairs={{0,4},{2,6},{4,0},{6,2},{8,12},{10,14},{12,8},{14,10},{1,5},{3,7},... | collective-permute-start | bytes 110600 | tf_op jit(solution)/shard_map/ppermute | solution.py:30
  14.1 19.3 %copy-start = (s32[1048576]{0:T(1024)S(1)}, s32[1048576]{0:T(1024)}, u32[]{:S(2)}) copy-start(s32[1048576]{0:T(1024)} %param.24) | copy-start | bytes 12582916
  14.2 8.2 %collective-permute-start.10 = (bf16[144,128]{1,0:T(8,128)(2,1)S(1)}, bf16[144,128]{1,0:T(8,128)(2,1)S(1)}, u32[]{:S(2)}, u32[]{:S(2)}) collective-permute-start(bf16[144,128]{1,0:T(8,128)(2,1)S(1)} %get-tuple-element.50), channel_id=1, source_target_pairs={{0,12},{2,14},{4,8},{6,10},{8,4},{10,6},{12,0},{14,2},{1,13},{3,15... | collective-permute-start | bytes 110600 | tf_op jit(solution)/shard_map/ppermute | solution.py:30
  17.8 5.3 %collective-permute-start.8 = (bf16[144,128]{1,0:T(8,128)(2,1)S(1)}, bf16[144,128]{1,0:T(8,128)(2,1)S(1)}, u32[]{:S(2)}, u32[]{:S(2)}) collective-permute-start(bf16[144,128]{1,0:T(8,128)(2,1)S(1)} %get-tuple-element.48), channel_id=1, source_target_pairs={{0,8},{2,10},{4,12},{6,14},{8,0},{10,2},{12,4},{14,6},{1,9},{3,11}... | collective-permute-start | bytes 110600 | tf_op jit(solution)/shard_map/ppermute | solution.py:30
  17.9 5.3 %collective-permute-start.9 = (bf16[144,128]{1,0:T(8,128)(2,1)S(1)}, bf16[144,128]{1,0:T(8,128)(2,1)S(1)}, u32[]{:S(2)}, u32[]{:S(2)}) collective-permute-start(bf16[144,128]{1,0:T(8,128)(2,1)S(1)} %get-tuple-element.49), channel_id=1, source_target_pairs={{0,4},{2,6},{4,0},{6,2},{8,12},{10,14},{12,8},{14,10},{1,5},{3,7},... | collective-permute-start | bytes 110600 | tf_op jit(solution)/shard_map/ppermute | solution.py:30
  18.7 8.2 %collective-permute-start.4 = (bf16[144,128]{1,0:T(8,128)(2,1)S(1)}, bf16[144,128]{1,0:T(8,128)(2,1)S(1)}, u32[]{:S(2)}, u32[]{:S(2)}) collective-permute-start(bf16[144,128]{1,0:T(8,128)(2,1)S(1)} %add_up.5.own), channel_id=1, source_target_pairs={{0,12},{2,14},{4,8},{6,10},{8,4},{10,6},{12,0},{14,2},{1,13},{3,15... | collective-permute-start | bytes 110600 | tf_op jit(solution)/shard_map/ppermute | solution.py:30
  22.3 5.5 %collective-permute-start.5 = (bf16[144,128]{1,0:T(8,128)(2,1)S(1)}, bf16[144,128]{1,0:T(8,128)(2,1)S(1)}, u32[]{:S(2)}, u32[]{:S(2)}) collective-permute-start(bf16[144,128]{1,0:T(8,128)(2,1)S(1)} %add_up.5.own), channel_id=1, source_target_pairs={{0,8},{2,10},{4,12},{6,14},{8,0},{10,2},{12,4},{14,6},{1,9},{3,11}... | collective-permute-start | bytes 110600 | tf_op jit(solution)/shard_map/ppermute | solution.py:30
  22.3 5.5 %collective-permute-start.6 = (bf16[144,128]{1,0:T(8,128)(2,1)S(1)}, bf16[144,128]{1,0:T(8,128)(2,1)S(1)}, u32[]{:S(2)}, u32[]{:S(2)}) collective-permute-start(bf16[144,128]{1,0:T(8,128)(2,1)S(1)} %add_up.5.own), channel_id=1, source_target_pairs={{0,4},{2,6},{4,0},{6,2},{8,12},{10,14},{12,8},{14,10},{1,5},{3,7},... | collective-permute-start | bytes 110600 | tf_op jit(solution)/shard_map/ppermute | solution.py:30
  23.2 6.8 %collective-permute-start.11 = (bf16[144,128]{1,0:T(8,128)(2,1)S(1)}, bf16[144,128]{1,0:T(8,128)(2,1)S(1)}, u32[]{:S(2)}, u32[]{:S(2)}) collective-permute-start(bf16[144,128]{1,0:T(8,128)(2,1)S(1)} %add_up.7.own), channel_id=1, source_target_pairs={{0,12},{2,14},{4,8},{6,10},{8,4},{10,6},{12,0},{14,2},{1,13},{3,15... | collective-permute-start | bytes 110600 | tf_op jit(solution)/shard_map/ppermute | solution.py:30
  26.8 4.9 %collective-permute-start.12 = (bf16[144,128]{1,0:T(8,128)(2,1)S(1)}, bf16[144,128]{1,0:T(8,128)(2,1)S(1)}, u32[]{:S(2)}, u32[]{:S(2)}) collective-permute-start(bf16[144,128]{1,0:T(8,128)(2,1)S(1)} %add_up.7.own), channel_id=1, source_target_pairs={{0,8},{2,10},{4,12},{6,14},{8,0},{10,2},{12,4},{14,6},{1,9},{3,11}... | collective-permute-start | bytes 110600 | tf_op jit(solution)/shard_map/ppermute | solution.py:30
  26.8 4.9 %collective-permute-start.13 = (bf16[144,128]{1,0:T(8,128)(2,1)S(1)}, bf16[144,128]{1,0:T(8,128)(2,1)S(1)}, u32[]{:S(2)}, u32[]{:S(2)}) collective-permute-start(bf16[144,128]{1,0:T(8,128)(2,1)S(1)} %add_up.7.own), channel_id=1, source_target_pairs={{0,4},{2,6},{4,0},{6,2},{8,12},{10,14},{12,8},{14,10},{1,5},{3,7},... | collective-permute-start | bytes 110600 | tf_op jit(solution)/shard_map/ppermute | solution.py:30
  27.9 5.4 %collective-permute-start.15 = (bf16[576,128]{1,0:T(8,128)(2,1)S(1)}, bf16[576,128]{1,0:T(8,128)(2,1)S(1)}, u32[]{:S(2)}, u32[]{:S(2)}) collective-permute-start(bf16[576,128]{1,0:T(8,128)(2,1)S(1)} %join.2.refs_0_), channel_id=1, source_target_pairs={{0,2},{2,0},{4,6},{6,4},{8,10},{10,8},{12,14},{14,12},{1,3},{3,1},... | collective-permute-start | bytes 442376 | tf_op jit(solution)/shard_map/ppermute | solution.py:30
  31.7 5.2 %collective-permute-start.14 = (bf16[576,128]{1,0:T(8,128)(2,1)S(1)}, bf16[576,128]{1,0:T(8,128)(2,1)S(1)}, u32[]{:S(2)}, u32[]{:S(2)}) collective-permute-start(bf16[576,128]{1,0:T(8,128)(2,1)S(1)} %join.3.refs_0_), channel_id=1, source_target_pairs={{0,2},{2,0},{4,6},{6,4},{8,10},{10,8},{12,14},{14,12},{1,3},{3,1},... | collective-permute-start | bytes 442376 | tf_op jit(solution)/shard_map/ppermute | solution.py:30
  47.4 1.3 %collective-permute-start.16 = (f32[1,8192]{1,0:T(1,128)S(1)}, f32[1,8192]{1,0:T(1,128)S(1)}, u32[]{:S(2)}, u32[]{:S(2)}) collective-permute-start(f32[1,8192]{1,0:T(1,128)S(1)} %sampled.1), channel_id=1, source_target_pairs={{0,1},{1,0},{2,3},{3,2},{4,5},{5,4},{6,7},{7,6},{8,9},{9,8},{10,11... | collective-permute-start | bytes 98312 | tf_op jit(solution)/shard_map/ppermute | solution.py:30
  48.7 6.8 %collective-permute-start.17 = (f32[1,8192]{1,0:T(1,128)S(1)}, f32[1,8192]{1,0:T(1,128)S(1)}, u32[]{:S(2)}, u32[]{:S(2)}) collective-permute-start(f32[1,8192]{1,0:T(1,128)S(1)} %add.15), channel_id=1, source_target_pairs={{1,8},{3,10},{5,12},{7,14},{9,0},{11,2},{13,4},{15,6},{0,9},{2,11}... | collective-permute-start | bytes 98312 | tf_op jit(solution)/shard_map/ppermute | solution.py:275
  50.5 5.0 %collective-permute-start.18 = (f32[1,8192]{1,0:T(1,128)S(1)}, f32[1,8192]{1,0:T(1,128)S(1)}, u32[]{:S(2)}, u32[]{:S(2)}) collective-permute-start(f32[1,8192]{1,0:T(1,128)S(1)} %add.15), channel_id=1, source_target_pairs={{1,2},{3,0},{5,6},{7,4},{9,10},{11,8},{13,14},{15,12},{0,11},{2,9}... | collective-permute-start | bytes 98312 | tf_op jit(solution)/shard_map/ppermute | solution.py:275
  52.1 3.4 %collective-permute-start.19 = (f32[1,8192]{1,0:T(1,128)S(1)}, f32[1,8192]{1,0:T(1,128)S(1)}, u32[]{:S(2)}, u32[]{:S(2)}) collective-permute-start(f32[1,8192]{1,0:T(1,128)S(1)} %add.15), channel_id=1, source_target_pairs={{1,4},{3,6},{5,0},{7,2},{9,12},{11,14},{13,8},{15,10},{0,13},{2,15... | collective-permute-start | bytes 98312 | tf_op jit(solution)/shard_map/ppermute | solution.py:275
  52.1 5.0 %collective-permute-start.20 = (f32[1,8192]{1,0:T(1,128)S(1)}, f32[1,8192]{1,0:T(1,128)S(1)}, u32[]{:S(2)}, u32[]{:S(2)}) collective-permute-start(f32[1,8192]{1,0:T(1,128)S(1)} %add.15), channel_id=1, source_target_pairs={{1,6},{3,4},{5,2},{7,0},{9,14},{11,12},{13,10},{15,8},{0,15},{2,13... | collective-permute-start | bytes 98312 | tf_op jit(solution)/shard_map/ppermute | solution.py:275
  57.2 2.1 %collective-permute-start.21 = (f32[1,8192]{1,0:T(1,128)S(1)}, f32[1,8192]{1,0:T(1,128)S(1)}, u32[]{:S(2)}, u32[]{:S(2)}) collective-permute-start(f32[1,8192]{1,0:T(1,128)S(1)} %fusion.1), channel_id=1, source_target_pairs={{0,1},{1,0},{2,3},{3,2},{4,5},{5,4},{6,7},{7,6},{8,9},{9,8},{10,11... | collective-permute-start | bytes 98312 | tf_op jit(solution)/shard_map/ppermute | solution.py:30

commit v2 on v1

--- a/solution.py
+++ b/solution.py
@@ -85,7 +85,7 @@
     digit = my_digit(stage)
     size = own.shape[0]
     table[pl.ds(pl.multiple_of(digit * size, 16), size), :] = own[...]
-    for step, other in enumerate(others[::-1], 1):
+    for step, other in enumerate(others, 1):
         table[pl.ds(pl.multiple_of((digit ^ step) * size, 16), size), :] = other[...]
 
 
@@ -230,7 +230,7 @@
 
 def swap(sends, stage):
     return [
-        exchange(sends[step - 1], "coord", step << stage[0]) for step in range(stage[1] - 1, 0, -1)
+        exchange(sends[step - 1], "coord", step << stage[0]) for step in range(1, stage[1])
     ]
 
 
@@ -238,25 +238,20 @@
     return lax.optimization_barrier((first, second))[1]
 
 
-def all_sums(halves, stages, ahead):
-    beside = []
+def all_sums(halves, stages):
     owns = [half[0] for half in halves]
     sends = [half[1:] for half in halves]
     for stage, following in zip(stages, stages[1:] + [None], strict=True):
         got = [swap(send, stage) for send in sends]
         for i in range(len(owns)):
             own = after(owns[0], owns[i]) if i else owns[i]
-            order = got[i][1:] + got[i][:1] if i else got[i]
-            owns[i], *sends[i] = add_up(own, order, following)
+            owns[i], *sends[i] = add_up(own, got[i][::-1], following)
     for stage in stages[:0:-1]:
         got = [swap([own] * (stage[1] - 1), stage) for own in owns]
         for i in range(len(owns)):
             own = after(owns[0], owns[i]) if i else owns[i]
-            if stage is stages[1]:
-                beside.append(ahead[i](owns[0]))
-                own = after(beside[i], own)
             owns[i] = join(own, got[i], stage)
-    return beside, [[own] + swap([own] * (stages[0][1] - 1), stages[0]) for own in owns]
+    return [[own] + swap([own] * (stages[0][1] - 1), stages[0]) for own in owns]
 
 
 def total_over(contrib, count):
@@ -268,7 +263,7 @@
         radix = min(8, count >> shift)
         half = radix // 2
         terms = []
-        for step in range(half):
+        for step in range(half - 1, -1, -1):
             nearer, further = (step or half) << shift, (half + step) << shift
             pairs = [(2 * c + 1, 2 * (c ^ nearer)) for c in range(count)]
             pairs += [(2 * c, 2 * (c ^ further) + 1) for c in range(count)]
@@ -547,11 +542,9 @@
     )
     flags = after(long[0], flags)
     bits = (length * rank).bit_length() - 1
-    ahead = (
-        lambda ready: turn(x, go),
-        lambda ready: signs_of(rank, bits, after(ready, index)),
-    )
-    ((x_t, go_t), signs), (short, long) = all_sums([short, long], stages, ahead)
+    short, long = all_sums([short, long], stages)
+    x_t, go_t = turn(after(long[0], x), go)
+    signs = signs_of(rank, bits, after(long[0], index))
     wide_mix = wide(aligned, block, first, stages[0], short, gg, gu, h, flags)
     final_scale = adapter_scale * float(total) ** -0.5
     mix = along_rows(aligned, block, stages[0], length, long, x_t, go_t, wide_mix, flags)

time: 60.1 us -> 60.1 us (level)
  no operation moved by 1% of the time
where the time goes in v2:
time: 60.1 us; the launch traced here: 60 us
  starting transfers between devices  32.3 us (54%)
  Pallas kernels  19 us (32%)
  waiting for transfers between devices  7.77 us (13%)
  other arithmetic  0.77 us (1%)
    ppermute x18, starting transfers between devices, exchange(): return lax.ppermute(value, axis, pairs)  25.5 us
    pallas_call x1, Pallas kernels, picked(): pl.pallas_call(pick_kernel, out_shape=jax.ShapeDtypeStruct((where.shape[0...  7.63 us
    ppermute x4, starting transfers between devices, total_over(): got = lax.ppermute(total, ('coord', 'ckpt'), pairs)  6.82 us
    ppermute x18, waiting for transfers between devices, exchange(): return lax.ppermute(value, axis, pairs)  6.17 us
    pallas_call x1, Pallas kernels, long_products(): pl.pallas_call(functools.partial(long_kernel, stage, cut), out_shape=shap...  3.76 us
    pallas_call x1, Pallas kernels, wide(): pl.pallas_call(functools.partial(wide_kernel, aligned, block, first, stag...  1.98 us
    pallas_call x1, Pallas kernels, short_products(): pl.pallas_call(functools.partial(short_kernel, stage, cuts), out_shape=sh...  1.9 us
    ppermute x4, waiting for transfers between devices, total_over(): got = lax.ppermute(total, ('coord', 'ckpt'), pairs)  1.59 us
  transfers between devices with their start and end apart: 22, of which 7 were waited for; matrix products, arithmetic and copies ran while one was open for 0% of the time, Pallas kernels for 11%

profile of v2, /device:TPU:0, one launch (start us, length us, event | category | flops | bytes accessed | tf_op | source)
XLA Modules:
  0.0 60.0 jit_solution(11485053945560488633)
XLA Ops:
  0.0 1.9 %short.1 = (bf16[384,512]{1,0:T(8,128)(2,1)S(1)}, bf16[384,512]{1,0:T(8,128)(2,1)S(1)}, f32[576,128]{1,0:T(8,128)S(1)}, bf16[576,128]{1,0:T(8,128)(2,1)S(1)}) custom-call(bf16[384,512]{1,0:T(8,128)(2,1)} %bitcast.22, bf16[384,512]{1,0:T(8,128)(2,1)} %bitcast.23, bf16[512,128]{1,0:T(8,128)(2,1)} %bitcast.24, bf16[512,128]{1,0:T(8,128)(2,1)} %bitcast.25, ...), custom_call_target="tpu_custom_call" | custom-call | flops 100000000 | bytes 6000000 | tf_op jit(solution)/shard_map/short/pallas_call | solution.py:123
  1.9 3.1 %collective-permute-start = (bf16[576,128]{1,0:T(8,128)(2,1)S(1)}, bf16[576,128]{1,0:T(8,128)(2,1)S(1)}, u32[]{:S(2)}, u32[]{:S(2)}) collective-permute-start(bf16[576,128]{1,0:T(8,128)(2,1)S(1)} %get-tuple-element.31), channel_id=1, source_target_pairs={{0,2},{2,0},{4,6},{6,4},{8,10},{10,8},{12,14},{14,12},{1,3},{3,1},... | collective-permute-start | bytes 442376 | tf_op jit(solution)/shard_map/ppermute | solution.py:30
  5.0 3.8 %long.1 = (bf16[1792,384]{1,0:T(8,128)(2,1)S(1)}, bf16[1792,384]{1,0:T(8,128)(2,1)S(1)}, bf16[1792,384]{1,0:T(8,128)(2,1)S(1)}, f32[576,128]{1,0:T(8,128)S(1)}, bf16[576,128]{1,0:T(8,128)(2,1)S(1)}) custom-call(bf16[1792,384]{1,0:T(8,128)(2,1)} %bitcast.16, bf16[1792,384]{1,0:T(8,128)(2,1)} %bitcast.17, bf16[1792,384]{1,0:T(8,128)(2,1)} %bitcast.18, ...), custom_call_target="tpu_custom_call" | custom-call | flops 1000000000 | bytes 8000000 | tf_op jit(solution)/shard_map/long/pallas_call | solution.py:174
  8.7 0.0 copy-start.1
  8.8 0.1 collective-permute-start.7
  8.9 0.0 collective-permute-done.refs_1_
  8.9 0.1 add_up.4
  8.9 4.1 %collective-permute-start.1 = (bf16[144,128]{1,0:T(8,128)(2,1)S(1)}, bf16[144,128]{1,0:T(8,128)(2,1)S(1)}, u32[]{:S(2)}, u32[]{:S(2)}) collective-permute-start(bf16[144,128]{1,0:T(8,128)(2,1)S(1)} %get-tuple-element.33), channel_id=1, source_target_pairs={{0,12},{2,14},{4,8},{6,10},{8,4},{10,6},{12,0},{14,2},{1,13},{3,15... | collective-permute-start | bytes 110600 | tf_op jit(solution)/shard_map/ppermute | solution.py:30
  13.1 0.0 collective-permute-start.2
  13.1 0.6 %collective-permute-start.3 = (bf16[144,128]{1,0:T(8,128)(2,1)S(1)}, bf16[144,128]{1,0:T(8,128)(2,1)S(1)}, u32[]{:S(2)}, u32[]{:S(2)}) collective-permute-start(bf16[144,128]{1,0:T(8,128)(2,1)S(1)} %get-tuple-element.35), channel_id=1, source_target_pairs={{0,4},{2,6},{4,0},{6,2},{8,12},{10,14},{12,8},{14,10},{1,5},{3,7},... | collective-permute-start | bytes 110600 | tf_op jit(solution)/shard_map/ppermute | solution.py:30
  13.7 0.4 collective-permute-done.7.refs_1_
  14.1 0.0 copy-start
  14.2 3.7 %collective-permute-start.8 = (bf16[144,128]{1,0:T(8,128)(2,1)S(1)}, bf16[144,128]{1,0:T(8,128)(2,1)S(1)}, u32[]{:S(2)}, u32[]{:S(2)}) collective-permute-start(bf16[144,128]{1,0:T(8,128)(2,1)S(1)} %get-tuple-element.41), channel_id=1, source_target_pairs={{0,12},{2,14},{4,8},{6,10},{8,4},{10,6},{12,0},{14,2},{1,13},{3,15... | collective-permute-start | bytes 110600 | tf_op jit(solution)/shard_map/ppermute | solution.py:30
  17.8 0.0 collective-permute-start.9
  17.8 0.0 collective-permute-done.1.refs_1_
  17.9 0.8 %collective-permute-start.10 = (bf16[144,128]{1,0:T(8,128)(2,1)S(1)}, bf16[144,128]{1,0:T(8,128)(2,1)S(1)}, u32[]{:S(2)}, u32[]{:S(2)}) collective-permute-start(bf16[144,128]{1,0:T(8,128)(2,1)S(1)} %get-tuple-element.43), channel_id=1, source_target_pairs={{0,4},{2,6},{4,0},{6,2},{8,12},{10,14},{12,8},{14,10},{1,5},{3,7},... | collective-permute-start | bytes 110600 | tf_op jit(solution)/shard_map/ppermute | solution.py:30
  18.6 0.0 collective-permute-done.2.refs_2_
  18.6 0.0 collective-permute-done.3.refs_3_
  18.7 3.7 %collective-permute-start.6 = (bf16[144,128]{1,0:T(8,128)(2,1)S(1)}, bf16[144,128]{1,0:T(8,128)(2,1)S(1)}, u32[]{:S(2)}, u32[]{:S(2)}) collective-permute-start(bf16[144,128]{1,0:T(8,128)(2,1)S(1)} %add_up.5.own), channel_id=1, source_target_pairs={{0,12},{2,14},{4,8},{6,10},{8,4},{10,6},{12,0},{14,2},{1,13},{3,15... | collective-permute-start | bytes 110600 | tf_op jit(solution)/shard_map/ppermute | solution.py:30
  22.3 0.0 collective-permute-start.5
  22.3 0.0 collective-permute-done.8.refs_1_
  22.3 0.8 %collective-permute-start.4 = (bf16[144,128]{1,0:T(8,128)(2,1)S(1)}, bf16[144,128]{1,0:T(8,128)(2,1)S(1)}, u32[]{:S(2)}, u32[]{:S(2)}) collective-permute-start(bf16[144,128]{1,0:T(8,128)(2,1)S(1)} %add_up.5.own), channel_id=1, source_target_pairs={{0,4},{2,6},{4,0},{6,2},{8,12},{10,14},{12,8},{14,10},{1,5},{3,7},... | collective-permute-start | bytes 110600 | tf_op jit(solution)/shard_map/ppermute | solution.py:30
  23.1 0.0 collective-permute-done.9.refs_2_
  23.1 0.0 collective-permute-done.10.refs_3_
  23.2 3.7 %collective-permute-start.13 = (bf16[144,128]{1,0:T(8,128)(2,1)S(1)}, bf16[144,128]{1,0:T(8,128)(2,1)S(1)}, u32[]{:S(2)}, u32[]{:S(2)}) collective-permute-start(bf16[144,128]{1,0:T(8,128)(2,1)S(1)} %add_up.7.own), channel_id=1, source_target_pairs={{0,12},{2,14},{4,8},{6,10},{8,4},{10,6},{12,0},{14,2},{1,13},{3,15... | collective-permute-start | bytes 110600 | tf_op jit(solution)/shard_map/ppermute | solution.py:30
  26.8 0.0 collective-permute-start.12
  26.8 0.0 collective-permute-done.6.refs_2_
  26.8 0.8 %collective-permute-start.11 = (bf16[144,128]{1,0:T(8,128)(2,1)S(1)}, bf16[144,128]{1,0:T(8,128)(2,1)S(1)}, u32[]{:S(2)}, u32[]{:S(2)}) collective-permute-start(bf16[144,128]{1,0:T(8,128)(2,1)S(1)} %add_up.7.own), channel_id=1, source_target_pairs={{0,4},{2,6},{4,0},{6,2},{8,12},{10,14},{12,8},{14,10},{1,5},{3,7},... | collective-permute-start | bytes 110600 | tf_op jit(solution)/shard_map/ppermute | solution.py:30
  27.6 0.0 collective-permute-done.5.refs_1_
  27.6 0.0 collective-permute-done.4.refs_0_
  27.7 1.5 %collective-permute-start.15 = (bf16[576,128]{1,0:T(8,128)(2,1)S(1)}, bf16[576,128]{1,0:T(8,128)(2,1)S(1)}, u32[]{:S(2)}, u32[]{:S(2)}) collective-permute-start(bf16[576,128]{1,0:T(8,128)(2,1)S(1)} %join.2.refs_0_), channel_id=1, source_target_pairs={{0,2},{2,0},{4,6},{6,4},{8,10},{10,8},{12,14},{14,12},{1,3},{3,1},... | collective-permute-start | bytes 442376 | tf_op jit(solution)/shard_map/ppermute | solution.py:30
  29.2 0.2 collective-permute-done.13.refs_2_
  29.4 2.3 %collective-permute-done.12.refs_1_ = bf16[144,128]{1,0:T(8,128)(2,1)S(1)} collective-permute-done((bf16[144,128]{1,0:T(8,128)(2,1)S(1)}, bf16[144,128]{1,0:T(8,128)(2,1)S(1)}, u32[]{:S(2)}, u32[]{:S(2)}) %collective-permute-start.12) | collective-permute-done | bytes 36896 | tf_op jit(solution)/shard_map/ppermute | solution.py:30
  31.7 0.0 collective-permute-done.11.refs_0_
  31.7 1.3 %collective-permute-start.14 = (bf16[576,128]{1,0:T(8,128)(2,1)S(1)}, bf16[576,128]{1,0:T(8,128)(2,1)S(1)}, u32[]{:S(2)}, u32[]{:S(2)}) collective-permute-start(bf16[576,128]{1,0:T(8,128)(2,1)S(1)} %join.3.refs_0_), channel_id=1, source_target_pairs={{0,2},{2,0},{4,6},{6,4},{8,10},{10,8},{12,14},{14,12},{1,3},{3,1},... | collective-permute-start | bytes 442376 | tf_op jit(solution)/shard_map/ppermute | solution.py:30
  33.0 0.0 copy-done.1
  33.0 0.5 signs.1
  33.5 0.3 turn.1
  33.8 0.0 collective-permute-done.15.refs_1_
  33.8 0.0 copy-done
  33.8 2.0 %wide.1.refs_4_ = f32[5376,128]{1,0:T(8,128)S(1)} custom-call(bf16[576,128]{1,0:T(8,128)(2,1)S(1)} %join.2.refs_0_, bf16[576,128]{1,0:T(8,128)(2,1)S(1)} %collective-permute-done.15.refs_1_, bf16[1792,384]{1,0:T(8,128)(2,1)S(1)} %get-tuple-element.50.refs_2_, bf16[1792,384]{1,0:T(8,128)(2,1)S(1)} %get-tuple-element.51.refs_3_, ...), custom_call_target="tpu_custom_call" | custom-call | flops 1000000000 | bytes 10000000 | tf_op jit(solution)/shard_map/wide/pallas_call | solution.py:352
  35.8 1.1 %collective-permute-done.14.refs_1_ = bf16[576,128]{1,0:T(8,128)(2,1)S(1)} collective-permute-done((bf16[576,128]{1,0:T(8,128)(2,1)S(1)}, bf16[576,128]{1,0:T(8,128)(2,1)S(1)}, u32[]{:S(2)}, u32[]{:S(2)}) %collective-permute-start.14) | collective-permute-done | bytes 147488 | tf_op jit(solution)/shard_map/ppermute | solution.py:30
  36.9 1.5 %along_rows.1.mix = f32[8192,128]{1,0:T(8,128)S(1)} custom-call(bf16[576,128]{1,0:T(8,128)(2,1)S(1)} %join.3.refs_0_, bf16[576,128]{1,0:T(8,128)(2,1)S(1)} %collective-permute-done.14.refs_1_, bf16[512,384]{1,0:T(8,128)(2,1)S(1)} %get-tuple-element.48.refs_2_, bf16[512,384]{1,0:T(8,128)(2,1)S(1)} %get-tuple-element.49.refs_3_, f32[5376,128]{1,0:T(8,128)S(1)} %wide.1.refs_4_, ...), custom_call_target="tpu_custom_call" | custom-call | tf_op jit(solution)/shard_map/along_rows/pallas_call | solution.py:409
  38.5 7.6 %picked.1.rows = f32[8192,128]{1,0:T(8,128)S(1)} custom-call(f32[8192,128]{1,0:T(8,128)S(1)} %along_rows.1.mix, s32[8192]{0:T(1024)S(1)} %and_or_fusion.where), custom_call_target="tpu_custom_call" | custom-call | tf_op jit(solution)/shard_map/picked/pallas_call | solution.py:483
  46.1 1.3 %sampled.1 = f32[1,8192]{1,0:T(1,128)S(1)} custom-call(f32[8192,128]{1,0:T(8,128)S(1)} %picked.1.rows, bf16[128,8192]{1,0:T(8,128)(2,1)S(1)} %signs.1), custom_call_target="tpu_custom_call" | custom-call | tf_op jit(solution)/shard_map/sampled/pallas_call | solution.py:510
  47.4 0.1 collective-permute-start.16
  47.4 1.2 %collective-permute-done.16 = f32[1,8192]{1,0:T(1,128)S(1)} collective-permute-done((f32[1,8192]{1,0:T(1,128)S(1)}, f32[1,8192]{1,0:T(1,128)S(1)}, u32[]{:S(2)}, u32[]{:S(2)}) %collective-permute-start.16) | collective-permute-done | bytes 32800 | tf_op jit(solution)/shard_map/ppermute | solution.py:30
  48.7 1.9 %collective-permute-start.20 = (f32[1,8192]{1,0:T(1,128)S(1)}, f32[1,8192]{1,0:T(1,128)S(1)}, u32[]{:S(2)}, u32[]{:S(2)}) collective-permute-start(f32[1,8192]{1,0:T(1,128)S(1)} %add.15), channel_id=1, source_target_pairs={{1,8},{3,10},{5,12},{7,14},{9,0},{11,2},{13,4},{15,6},{0,9},{2,11}... | collective-permute-start | bytes 98312 | tf_op jit(solution)/shard_map/ppermute | solution.py:270
  50.5 1.5 %collective-permute-start.19 = (f32[1,8192]{1,0:T(1,128)S(1)}, f32[1,8192]{1,0:T(1,128)S(1)}, u32[]{:S(2)}, u32[]{:S(2)}) collective-permute-start(f32[1,8192]{1,0:T(1,128)S(1)} %add.15), channel_id=1, source_target_pairs={{1,2},{3,0},{5,6},{7,4},{9,10},{11,8},{13,14},{15,12},{0,11},{2,9}... | collective-permute-start | bytes 98312 | tf_op jit(solution)/shard_map/ppermute | solution.py:270
  52.1 0.0 collective-permute-start.18
  52.1 3.4 %collective-permute-start.17 = (f32[1,8192]{1,0:T(1,128)S(1)}, f32[1,8192]{1,0:T(1,128)S(1)}, u32[]{:S(2)}, u32[]{:S(2)}) collective-permute-start(f32[1,8192]{1,0:T(1,128)S(1)} %add.15), channel_id=1, source_target_pairs={{1,6},{3,4},{5,2},{7,0},{9,14},{11,12},{13,10},{15,8},{0,15},{2,13... | collective-permute-start | bytes 98312 | tf_op jit(solution)/shard_map/ppermute | solution.py:270
  55.5 0.0 collective-permute-done.20
  55.5 0.0 collective-permute-done.19
  55.5 0.0 collective-permute-done.18
  55.5 1.6 %collective-permute-done.17 = f32[1,8192]{1,0:T(1,128)S(1)} collective-permute-done((f32[1,8192]{1,0:T(1,128)S(1)}, f32[1,8192]{1,0:T(1,128)S(1)}, u32[]{:S(2)}, u32[]{:S(2)}) %collective-permute-start.17) | collective-permute-done | bytes 32800 | tf_op jit(solution)/shard_map/ppermute | solution.py:270
  57.1 0.1 fusion.1
  57.2 1.3 %collective-permute-start.21 = (f32[1,8192]{1,0:T(1,128)S(1)}, f32[1,8192]{1,0:T(1,128)S(1)}, u32[]{:S(2)}, u32[]{:S(2)}) collective-permute-start(f32[1,8192]{1,0:T(1,128)S(1)} %fusion.1), channel_id=1, source_target_pairs={{0,1},{1,0},{2,3},{3,2},{4,5},{5,4},{6,7},{7,6},{8,9},{9,8},{10,11... | collective-permute-start | bytes 98312 | tf_op jit(solution)/shard_map/ppermute | solution.py:30
  58.5 0.9 %collective-permute-done.21 = f32[1,8192]{1,0:T(1,128)S(1)} collective-permute-done((f32[1,8192]{1,0:T(1,128)S(1)}, f32[1,8192]{1,0:T(1,128)S(1)}, u32[]{:S(2)}, u32[]{:S(2)}) %collective-permute-start.21) | collective-permute-done | bytes 32800 | tf_op jit(solution)/shard_map/ppermute | solution.py:30
  59.3 0.6 %add.19 = f32[1,8192]{1,0:T(1,128)} add(f32[1,8192]{1,0:T(1,128)S(1)} %fusion.1, f32[1,8192]{1,0:T(1,128)S(1)} %collective-permute-done.21) | non-fusion elementwise | flops 8192 | bytes 98304 | tf_op jit(solution)/shard_map/add | solution.py:274
  (7 shorter events, 0.2 us)
Async XLA Ops:
  1.9 7.0 %collective-permute-start = (bf16[576,128]{1,0:T(8,128)(2,1)S(1)}, bf16[576,128]{1,0:T(8,128)(2,1)S(1)}, u32[]{:S(2)}, u32[]{:S(2)}) collective-permute-start(bf16[576,128]{1,0:T(8,128)(2,1)S(1)} %get-tuple-element.31), channel_id=1, source_target_pairs={{0,2},{2,0},{4,6},{6,4},{8,10},{10,8},{12,14},{14,12},{1,3},{3,1},... | collective-permute-start | bytes 442376 | tf_op jit(solution)/shard_map/ppermute | solution.py:30
  8.7 24.3 %copy-start.1 = (s32[8192]{0:T(1024)S(1)}, s32[8192]{0:T(1024)}, u32[]{:S(2)}) copy-start(s32[8192]{0:T(1024)} %param.25) | copy-start | bytes 98308
  8.8 5.4 %collective-permute-start.7 = (bf16[576,128]{1,0:T(8,128)(2,1)S(1)}, bf16[576,128]{1,0:T(8,128)(2,1)S(1)}, u32[]{:S(2)}, u32[]{:S(2)}) collective-permute-start(bf16[576,128]{1,0:T(8,128)(2,1)S(1)} %get-tuple-element.38), channel_id=1, source_target_pairs={{0,2},{2,0},{4,6},{6,4},{8,10},{10,8},{12,14},{14,12},{1,3},{3,1},... | collective-permute-start | bytes 442376 | tf_op jit(solution)/shard_map/ppermute | solution.py:30
  8.9 8.9 %collective-permute-start.1 = (bf16[144,128]{1,0:T(8,128)(2,1)S(1)}, bf16[144,128]{1,0:T(8,128)(2,1)S(1)}, u32[]{:S(2)}, u32[]{:S(2)}) collective-permute-start(bf16[144,128]{1,0:T(8,128)(2,1)S(1)} %get-tuple-element.33), channel_id=1, source_target_pairs={{0,12},{2,14},{4,8},{6,10},{8,4},{10,6},{12,0},{14,2},{1,13},{3,15... | collective-permute-start | bytes 110600 | tf_op jit(solution)/shard_map/ppermute | solution.py:30
  13.1 5.6 %collective-permute-start.2 = (bf16[144,128]{1,0:T(8,128)(2,1)S(1)}, bf16[144,128]{1,0:T(8,128)(2,1)S(1)}, u32[]{:S(2)}, u32[]{:S(2)}) collective-permute-start(bf16[144,128]{1,0:T(8,128)(2,1)S(1)} %get-tuple-element.34), channel_id=1, source_target_pairs={{0,8},{2,10},{4,12},{6,14},{8,0},{10,2},{12,4},{14,6},{1,9},{3,11}... | collective-permute-start | bytes 110600 | tf_op jit(solution)/shard_map/ppermute | solution.py:30
  13.1 5.6 %collective-permute-start.3 = (bf16[144,128]{1,0:T(8,128)(2,1)S(1)}, bf16[144,128]{1,0:T(8,128)(2,1)S(1)}, u32[]{:S(2)}, u32[]{:S(2)}) collective-permute-start(bf16[144,128]{1,0:T(8,128)(2,1)S(1)} %get-tuple-element.35), channel_id=1, source_target_pairs={{0,4},{2,6},{4,0},{6,2},{8,12},{10,14},{12,8},{14,10},{1,5},{3,7},... | collective-permute-start | bytes 110600 | tf_op jit(solution)/shard_map/ppermute | solution.py:30
  14.1 19.7 %copy-start = (s32[1048576]{0:T(1024)S(1)}, s32[1048576]{0:T(1024)}, u32[]{:S(2)}) copy-start(s32[1048576]{0:T(1024)} %param.24) | copy-start | bytes 12582916
  14.2 8.2 %collective-permute-start.8 = (bf16[144,128]{1,0:T(8,128)(2,1)S(1)}, bf16[144,128]{1,0:T(8,128)(2,1)S(1)}, u32[]{:S(2)}, u32[]{:S(2)}) collective-permute-start(bf16[144,128]{1,0:T(8,128)(2,1)S(1)} %get-tuple-element.41), channel_id=1, source_target_pairs={{0,12},{2,14},{4,8},{6,10},{8,4},{10,6},{12,0},{14,2},{1,13},{3,15... | collective-permute-start | bytes 110600 | tf_op jit(solution)/shard_map/ppermute | solution.py:30
  17.8 5.3 %collective-permute-start.9 = (bf16[144,128]{1,0:T(8,128)(2,1)S(1)}, bf16[144,128]{1,0:T(8,128)(2,1)S(1)}, u32[]{:S(2)}, u32[]{:S(2)}) collective-permute-start(bf16[144,128]{1,0:T(8,128)(2,1)S(1)} %get-tuple-element.42), channel_id=1, source_target_pairs={{0,8},{2,10},{4,12},{6,14},{8,0},{10,2},{12,4},{14,6},{1,9},{3,11}... | collective-permute-start | bytes 110600 | tf_op jit(solution)/shard_map/ppermute | solution.py:30
  17.9 5.3 %collective-permute-start.10 = (bf16[144,128]{1,0:T(8,128)(2,1)S(1)}, bf16[144,128]{1,0:T(8,128)(2,1)S(1)}, u32[]{:S(2)}, u32[]{:S(2)}) collective-permute-start(bf16[144,128]{1,0:T(8,128)(2,1)S(1)} %get-tuple-element.43), channel_id=1, source_target_pairs={{0,4},{2,6},{4,0},{6,2},{8,12},{10,14},{12,8},{14,10},{1,5},{3,7},... | collective-permute-start | bytes 110600 | tf_op jit(solution)/shard_map/ppermute | solution.py:30
  18.7 8.2 %collective-permute-start.6 = (bf16[144,128]{1,0:T(8,128)(2,1)S(1)}, bf16[144,128]{1,0:T(8,128)(2,1)S(1)}, u32[]{:S(2)}, u32[]{:S(2)}) collective-permute-start(bf16[144,128]{1,0:T(8,128)(2,1)S(1)} %add_up.5.own), channel_id=1, source_target_pairs={{0,12},{2,14},{4,8},{6,10},{8,4},{10,6},{12,0},{14,2},{1,13},{3,15... | collective-permute-start | bytes 110600 | tf_op jit(solution)/shard_map/ppermute | solution.py:30
  22.3 5.3 %collective-permute-start.5 = (bf16[144,128]{1,0:T(8,128)(2,1)S(1)}, bf16[144,128]{1,0:T(8,128)(2,1)S(1)}, u32[]{:S(2)}, u32[]{:S(2)}) collective-permute-start(bf16[144,128]{1,0:T(8,128)(2,1)S(1)} %add_up.5.own), channel_id=1, source_target_pairs={{0,8},{2,10},{4,12},{6,14},{8,0},{10,2},{12,4},{14,6},{1,9},{3,11}... | collective-permute-start | bytes 110600 | tf_op jit(solution)/shard_map/ppermute | solution.py:30
  22.3 5.3 %collective-permute-start.4 = (bf16[144,128]{1,0:T(8,128)(2,1)S(1)}, bf16[144,128]{1,0:T(8,128)(2,1)S(1)}, u32[]{:S(2)}, u32[]{:S(2)}) collective-permute-start(bf16[144,128]{1,0:T(8,128)(2,1)S(1)} %add_up.5.own), channel_id=1, source_target_pairs={{0,4},{2,6},{4,0},{6,2},{8,12},{10,14},{12,8},{14,10},{1,5},{3,7},... | collective-permute-start | bytes 110600 | tf_op jit(solution)/shard_map/ppermute | solution.py:30
  23.2 6.2 %collective-permute-start.13 = (bf16[144,128]{1,0:T(8,128)(2,1)S(1)}, bf16[144,128]{1,0:T(8,128)(2,1)S(1)}, u32[]{:S(2)}, u32[]{:S(2)}) collective-permute-start(bf16[144,128]{1,0:T(8,128)(2,1)S(1)} %add_up.7.own), channel_id=1, source_target_pairs={{0,12},{2,14},{4,8},{6,10},{8,4},{10,6},{12,0},{14,2},{1,13},{3,15... | collective-permute-start | bytes 110600 | tf_op jit(solution)/shard_map/ppermute | solution.py:30
  26.8 4.9 %collective-permute-start.12 = (bf16[144,128]{1,0:T(8,128)(2,1)S(1)}, bf16[144,128]{1,0:T(8,128)(2,1)S(1)}, u32[]{:S(2)}, u32[]{:S(2)}) collective-permute-start(bf16[144,128]{1,0:T(8,128)(2,1)S(1)} %add_up.7.own), channel_id=1, source_target_pairs={{0,8},{2,10},{4,12},{6,14},{8,0},{10,2},{12,4},{14,6},{1,9},{3,11}... | collective-permute-start | bytes 110600 | tf_op jit(solution)/shard_map/ppermute | solution.py:30
  26.8 4.9 %collective-permute-start.11 = (bf16[144,128]{1,0:T(8,128)(2,1)S(1)}, bf16[144,128]{1,0:T(8,128)(2,1)S(1)}, u32[]{:S(2)}, u32[]{:S(2)}) collective-permute-start(bf16[144,128]{1,0:T(8,128)(2,1)S(1)} %add_up.7.own), channel_id=1, source_target_pairs={{0,4},{2,6},{4,0},{6,2},{8,12},{10,14},{12,8},{14,10},{1,5},{3,7},... | collective-permute-start | bytes 110600 | tf_op jit(solution)/shard_map/ppermute | solution.py:30
  27.7 6.1 %collective-permute-start.15 = (bf16[576,128]{1,0:T(8,128)(2,1)S(1)}, bf16[576,128]{1,0:T(8,128)(2,1)S(1)}, u32[]{:S(2)}, u32[]{:S(2)}) collective-permute-start(bf16[576,128]{1,0:T(8,128)(2,1)S(1)} %join.2.refs_0_), channel_id=1, source_target_pairs={{0,2},{2,0},{4,6},{6,4},{8,10},{10,8},{12,14},{14,12},{1,3},{3,1},... | collective-permute-start | bytes 442376 | tf_op jit(solution)/shard_map/ppermute | solution.py:30
  31.7 5.2 %collective-permute-start.14 = (bf16[576,128]{1,0:T(8,128)(2,1)S(1)}, bf16[576,128]{1,0:T(8,128)(2,1)S(1)}, u32[]{:S(2)}, u32[]{:S(2)}) collective-permute-start(bf16[576,128]{1,0:T(8,128)(2,1)S(1)} %join.3.refs_0_), channel_id=1, source_target_pairs={{0,2},{2,0},{4,6},{6,4},{8,10},{10,8},{12,14},{14,12},{1,3},{3,1},... | collective-permute-start | bytes 442376 | tf_op jit(solution)/shard_map/ppermute | solution.py:30
  47.4 1.3 %collective-permute-start.16 = (f32[1,8192]{1,0:T(1,128)S(1)}, f32[1,8192]{1,0:T(1,128)S(1)}, u32[]{:S(2)}, u32[]{:S(2)}) collective-permute-start(f32[1,8192]{1,0:T(1,128)S(1)} %sampled.1), channel_id=1, source_target_pairs={{0,1},{1,0},{2,3},{3,2},{4,5},{5,4},{6,7},{7,6},{8,9},{9,8},{10,11... | collective-permute-start | bytes 98312 | tf_op jit(solution)/shard_map/ppermute | solution.py:30
  48.7 6.8 %collective-permute-start.20 = (f32[1,8192]{1,0:T(1,128)S(1)}, f32[1,8192]{1,0:T(1,128)S(1)}, u32[]{:S(2)}, u32[]{:S(2)}) collective-permute-start(f32[1,8192]{1,0:T(1,128)S(1)} %add.15), channel_id=1, source_target_pairs={{1,8},{3,10},{5,12},{7,14},{9,0},{11,2},{13,4},{15,6},{0,9},{2,11}... | collective-permute-start | bytes 98312 | tf_op jit(solution)/shard_map/ppermute | solution.py:270
  50.5 5.0 %collective-permute-start.19 = (f32[1,8192]{1,0:T(1,128)S(1)}, f32[1,8192]{1,0:T(1,128)S(1)}, u32[]{:S(2)}, u32[]{:S(2)}) collective-permute-start(f32[1,8192]{1,0:T(1,128)S(1)} %add.15), channel_id=1, source_target_pairs={{1,2},{3,0},{5,6},{7,4},{9,10},{11,8},{13,14},{15,12},{0,11},{2,9}... | collective-permute-start | bytes 98312 | tf_op jit(solution)/shard_map/ppermute | solution.py:270
  52.1 3.4 %collective-permute-start.18 = (f32[1,8192]{1,0:T(1,128)S(1)}, f32[1,8192]{1,0:T(1,128)S(1)}, u32[]{:S(2)}, u32[]{:S(2)}) collective-permute-start(f32[1,8192]{1,0:T(1,128)S(1)} %add.15), channel_id=1, source_target_pairs={{1,4},{3,6},{5,0},{7,2},{9,12},{11,14},{13,8},{15,10},{0,13},{2,15... | collective-permute-start | bytes 98312 | tf_op jit(solution)/shard_map/ppermute | solution.py:270
  52.1 5.0 %collective-permute-start.17 = (f32[1,8192]{1,0:T(1,128)S(1)}, f32[1,8192]{1,0:T(1,128)S(1)}, u32[]{:S(2)}, u32[]{:S(2)}) collective-permute-start(f32[1,8192]{1,0:T(1,128)S(1)} %add.15), channel_id=1, source_target_pairs={{1,6},{3,4},{5,2},{7,0},{9,14},{11,12},{13,10},{15,8},{0,15},{2,13... | collective-permute-start | bytes 98312 | tf_op jit(solution)/shard_map/ppermute | solution.py:270
  57.2 2.1 %collective-permute-start.21 = (f32[1,8192]{1,0:T(1,128)S(1)}, f32[1,8192]{1,0:T(1,128)S(1)}, u32[]{:S(2)}, u32[]{:S(2)}) collective-permute-start(f32[1,8192]{1,0:T(1,128)S(1)} %fusion.1), channel_id=1, source_target_pairs={{0,1},{1,0},{2,3},{3,2},{4,5},{5,4},{6,7},{7,6},{8,9},{9,8},{10,11... | collective-permute-start | bytes 98312 | tf_op jit(solution)/shard_map/ppermute | solution.py:30

commit v3 on v1

--- a/solution.py
+++ b/solution.py
@@ -149,15 +149,13 @@
         )
         waits.append(wait)
 
-    begin(0)
-    begin(1)
+    for slot in range(3):
+        begin(slot)
     row = 0
     for slot in range(3):
         waits[slot](0)
         adapter = adapters[slot][...].T
         waits[slot](1)
-        if slot == 0:
-            begin(2)
         value = dot(adapter, held[slot][...], ((1,), (0,)))
         for part in range(value.shape[1] // rank):
             table[row : row + rank, :] = value[:, part * rank : (part + 1) * rank]

time: 60.1 us -> 59.8 us (level)
  transfers between devices with their start and end apart: 22 -> 22, of which waited for: 7 -> 8; matrix products, arithmetic and copies ran while one was open for 0% -> 0% of each run, Pallas kernels for 11% -> 10%
where the time goes in v3:
time: 59.8 us; the launch traced here: 59.6 us
  starting transfers between devices  32.8 us (55%)
  Pallas kernels  18.4 us (31%)
  waiting for transfers between devices  7.46 us (12%)
  other arithmetic  0.77 us (1%)
    ppermute x18, starting transfers between devices, exchange(): return lax.ppermute(value, axis, pairs)  26 us
    pallas_call x1, Pallas kernels, picked(): pl.pallas_call(pick_kernel, out_shape=jax.ShapeDtypeStruct((where.shape[0...  7.63 us
    ppermute x4, starting transfers between devices, total_over(): got = lax.ppermute(total, ('coord', 'ckpt'), pairs)  6.82 us
    ppermute x18, waiting for transfers between devices, exchange(): return lax.ppermute(value, axis, pairs)  5.86 us
    pallas_call x1, Pallas kernels, long_products(): pl.pallas_call(functools.partial(long_kernel, stage, cut), out_shape=shap...  3.18 us
    pallas_call x1, Pallas kernels, wide(): pl.pallas_call(functools.partial(wide_kernel, aligned, block, first, stag...  1.98 us
    pallas_call x1, Pallas kernels, short_products(): pl.pallas_call(functools.partial(short_kernel, stage, cuts), out_shape=sh...  1.9 us
    ppermute x4, waiting for transfers between devices, total_over(): got = lax.ppermute(total, ('coord', 'ckpt'), pairs)  1.6 us
  transfers between devices with their start and end apart: 22, of which 8 were waited for; matrix products, arithmetic and copies ran while one was open for 0% of the time, Pallas kernels for 10%

profile of v3, /device:TPU:0, one launch (start us, length us, event | category | flops | bytes accessed | tf_op | source)
XLA Modules:
  0.0 59.6 jit_solution(1727003233403732656)
XLA Ops:
  0.0 1.9 %short.1 = (bf16[384,512]{1,0:T(8,128)(2,1)S(1)}, bf16[384,512]{1,0:T(8,128)(2,1)S(1)}, f32[576,128]{1,0:T(8,128)S(1)}, bf16[576,128]{1,0:T(8,128)(2,1)S(1)}) custom-call(bf16[384,512]{1,0:T(8,128)(2,1)} %bitcast.22, bf16[384,512]{1,0:T(8,128)(2,1)} %bitcast.23, bf16[512,128]{1,0:T(8,128)(2,1)} %bitcast.24, bf16[512,128]{1,0:T(8,128)(2,1)} %bitcast.25, ...), custom_call_target="tpu_custom_call" | custom-call | flops 100000000 | bytes 6000000 | tf_op jit(solution)/shard_map/short/pallas_call | solution.py:123
  1.9 3.1 %collective-permute-start = (bf16[576,128]{1,0:T(8,128)(2,1)S(1)}, bf16[576,128]{1,0:T(8,128)(2,1)S(1)}, u32[]{:S(2)}, u32[]{:S(2)}) collective-permute-start(bf16[576,128]{1,0:T(8,128)(2,1)S(1)} %get-tuple-element.36), channel_id=1, source_target_pairs={{0,2},{2,0},{4,6},{6,4},{8,10},{10,8},{12,14},{14,12},{1,3},{3,1},... | collective-permute-start | bytes 442376 | tf_op jit(solution)/shard_map/ppermute | solution.py:30
  5.0 3.2 %long.1 = (bf16[1792,384]{1,0:T(8,128)(2,1)S(1)}, bf16[1792,384]{1,0:T(8,128)(2,1)S(1)}, bf16[1792,384]{1,0:T(8,128)(2,1)S(1)}, f32[576,128]{1,0:T(8,128)S(1)}, bf16[576,128]{1,0:T(8,128)(2,1)S(1)}) custom-call(bf16[1792,384]{1,0:T(8,128)(2,1)} %bitcast.16, bf16[1792,384]{1,0:T(8,128)(2,1)} %bitcast.17, bf16[1792,384]{1,0:T(8,128)(2,1)} %bitcast.18, ...), custom_call_target="tpu_custom_call" | custom-call | flops 1000000000 | bytes 8000000 | tf_op jit(solution)/shard_map/long/pallas_call | solution.py:172
  8.2 0.0 copy-start.1
  8.2 0.1 collective-permute-start.7
  8.3 0.5 collective-permute-done.refs_1_
  8.9 3.9 %collective-permute-start.1 = (bf16[144,128]{1,0:T(8,128)(2,1)S(1)}, bf16[144,128]{1,0:T(8,128)(2,1)S(1)}, u32[]{:S(2)}, u32[]{:S(2)}) collective-permute-start(bf16[144,128]{1,0:T(8,128)(2,1)S(1)} %get-tuple-element.38), channel_id=1, source_target_pairs={{0,12},{2,14},{4,8},{6,10},{8,4},{10,6},{12,0},{14,2},{1,13},{3,15... | collective-permute-start | bytes 110600 | tf_op jit(solution)/shard_map/ppermute | solution.py:30
  12.7 0.0 collective-permute-start.2
  12.7 0.6 %collective-permute-start.3 = (bf16[144,128]{1,0:T(8,128)(2,1)S(1)}, bf16[144,128]{1,0:T(8,128)(2,1)S(1)}, u32[]{:S(2)}, u32[]{:S(2)}) collective-permute-start(bf16[144,128]{1,0:T(8,128)(2,1)S(1)} %get-tuple-element.40), channel_id=1, source_target_pairs={{0,4},{2,6},{4,0},{6,2},{8,12},{10,14},{12,8},{14,10},{1,5},{3,7},... | collective-permute-start | bytes 110600 | tf_op jit(solution)/shard_map/ppermute | solution.py:30
  13.4 0.2 collective-permute-done.7.refs_1_
  13.5 0.0 copy-start
  13.6 3.7 %collective-permute-start.10 = (bf16[144,128]{1,0:T(8,128)(2,1)S(1)}, bf16[144,128]{1,0:T(8,128)(2,1)S(1)}, u32[]{:S(2)}, u32[]{:S(2)}) collective-permute-start(bf16[144,128]{1,0:T(8,128)(2,1)S(1)} %get-tuple-element.50), channel_id=1, source_target_pairs={{0,12},{2,14},{4,8},{6,10},{8,4},{10,6},{12,0},{14,2},{1,13},{3,15... | collective-permute-start | bytes 110600 | tf_op jit(solution)/shard_map/ppermute | solution.py:30
  17.3 0.0 collective-permute-start.8
  17.3 0.0 collective-permute-done.1.refs_1_
  17.3 0.8 %collective-permute-start.9 = (bf16[144,128]{1,0:T(8,128)(2,1)S(1)}, bf16[144,128]{1,0:T(8,128)(2,1)S(1)}, u32[]{:S(2)}, u32[]{:S(2)}) collective-permute-start(bf16[144,128]{1,0:T(8,128)(2,1)S(1)} %get-tuple-element.49), channel_id=1, source_target_pairs={{0,4},{2,6},{4,0},{6,2},{8,12},{10,14},{12,8},{14,10},{1,5},{3,7},... | collective-permute-start | bytes 110600 | tf_op jit(solution)/shard_map/ppermute | solution.py:30
  18.0 0.0 collective-permute-done.2.refs_2_
  18.1 0.0 collective-permute-done.3.refs_3_
  18.1 3.7 %collective-permute-start.4 = (bf16[144,128]{1,0:T(8,128)(2,1)S(1)}, bf16[144,128]{1,0:T(8,128)(2,1)S(1)}, u32[]{:S(2)}, u32[]{:S(2)}) collective-permute-start(bf16[144,128]{1,0:T(8,128)(2,1)S(1)} %add_up.5.own), channel_id=1, source_target_pairs={{0,12},{2,14},{4,8},{6,10},{8,4},{10,6},{12,0},{14,2},{1,13},{3,15... | collective-permute-start | bytes 110600 | tf_op jit(solution)/shard_map/ppermute | solution.py:30
  21.8 0.0 collective-permute-start.5
  21.8 0.0 collective-permute-done.10.refs_3_
  21.8 0.8 %collective-permute-start.6 = (bf16[144,128]{1,0:T(8,128)(2,1)S(1)}, bf16[144,128]{1,0:T(8,128)(2,1)S(1)}, u32[]{:S(2)}, u32[]{:S(2)}) collective-permute-start(bf16[144,128]{1,0:T(8,128)(2,1)S(1)} %add_up.5.own), channel_id=1, source_target_pairs={{0,4},{2,6},{4,0},{6,2},{8,12},{10,14},{12,8},{14,10},{1,5},{3,7},... | collective-permute-start | bytes 110600 | tf_op jit(solution)/shard_map/ppermute | solution.py:30
  22.5 0.0 collective-permute-done.8.refs_1_
  22.5 0.0 collective-permute-done.9.refs_2_
  22.6 3.7 %collective-permute-start.11 = (bf16[144,128]{1,0:T(8,128)(2,1)S(1)}, bf16[144,128]{1,0:T(8,128)(2,1)S(1)}, u32[]{:S(2)}, u32[]{:S(2)}) collective-permute-start(bf16[144,128]{1,0:T(8,128)(2,1)S(1)} %add_up.7.own), channel_id=1, source_target_pairs={{0,12},{2,14},{4,8},{6,10},{8,4},{10,6},{12,0},{14,2},{1,13},{3,15... | collective-permute-start | bytes 110600 | tf_op jit(solution)/shard_map/ppermute | solution.py:30
  26.2 0.0 collective-permute-start.12
  26.2 0.0 collective-permute-done.4.refs_0_
  26.2 0.8 %collective-permute-start.13 = (bf16[144,128]{1,0:T(8,128)(2,1)S(1)}, bf16[144,128]{1,0:T(8,128)(2,1)S(1)}, u32[]{:S(2)}, u32[]{:S(2)}) collective-permute-start(bf16[144,128]{1,0:T(8,128)(2,1)S(1)} %add_up.7.own), channel_id=1, source_target_pairs={{0,4},{2,6},{4,0},{6,2},{8,12},{10,14},{12,8},{14,10},{1,5},{3,7},... | collective-permute-start | bytes 110600 | tf_op jit(solution)/shard_map/ppermute | solution.py:30
  27.0 0.3 turn.1
  27.3 0.0 collective-permute-done.5.refs_1_
  27.3 0.0 collective-permute-done.6.refs_2_
  27.3 1.8 %collective-permute-start.15 = (bf16[576,128]{1,0:T(8,128)(2,1)S(1)}, bf16[576,128]{1,0:T(8,128)(2,1)S(1)}, u32[]{:S(2)}, u32[]{:S(2)}) collective-permute-start(bf16[576,128]{1,0:T(8,128)(2,1)S(1)} %join.2.refs_0_), channel_id=1, source_target_pairs={{0,2},{2,0},{4,6},{6,4},{8,10},{10,8},{12,14},{14,12},{1,3},{3,1},... | collective-permute-start | bytes 442376 | tf_op jit(solution)/shard_map/ppermute | solution.py:30
  29.1 0.0 copy-done.1
  29.1 0.5 signs.1
  29.6 0.0 collective-permute-done.11.refs_0_
  29.6 1.5 %collective-permute-done.12.refs_1_ = bf16[144,128]{1,0:T(8,128)(2,1)S(1)} collective-permute-done((bf16[144,128]{1,0:T(8,128)(2,1)S(1)}, bf16[144,128]{1,0:T(8,128)(2,1)S(1)}, u32[]{:S(2)}, u32[]{:S(2)}) %collective-permute-start.12) | collective-permute-done | bytes 36896 | tf_op jit(solution)/shard_map/ppermute | solution.py:30
  31.1 0.0 collective-permute-done.13.refs_2_
  31.1 1.6 %collective-permute-start.14 = (bf16[576,128]{1,0:T(8,128)(2,1)S(1)}, bf16[576,128]{1,0:T(8,128)(2,1)S(1)}, u32[]{:S(2)}, u32[]{:S(2)}) collective-permute-start(bf16[576,128]{1,0:T(8,128)(2,1)S(1)} %join.3.refs_0_), channel_id=1, source_target_pairs={{0,2},{2,0},{4,6},{6,4},{8,10},{10,8},{12,14},{14,12},{1,3},{3,1},... | collective-permute-start | bytes 442376 | tf_op jit(solution)/shard_map/ppermute | solution.py:30
  32.8 0.0 collective-permute-done.15.refs_1_
  32.8 0.0 copy-done
  32.8 2.0 %wide.1.refs_4_ = f32[5376,128]{1,0:T(8,128)S(1)} custom-call(bf16[576,128]{1,0:T(8,128)(2,1)S(1)} %join.2.refs_0_, bf16[576,128]{1,0:T(8,128)(2,1)S(1)} %collective-permute-done.15.refs_1_, bf16[1792,384]{1,0:T(8,128)(2,1)S(1)} %get-tuple-element.53.refs_2_, bf16[1792,384]{1,0:T(8,128)(2,1)S(1)} %get-tuple-element.54.refs_3_, ...), custom_call_target="tpu_custom_call" | custom-call | flops 1000000000 | bytes 10000000 | tf_op jit(solution)/shard_map/wide/pallas_call | solution.py:355
  34.8 1.6 %collective-permute-done.14.refs_1_ = bf16[576,128]{1,0:T(8,128)(2,1)S(1)} collective-permute-done((bf16[576,128]{1,0:T(8,128)(2,1)S(1)}, bf16[576,128]{1,0:T(8,128)(2,1)S(1)}, u32[]{:S(2)}, u32[]{:S(2)}) %collective-permute-start.14) | collective-permute-done | bytes 147488 | tf_op jit(solution)/shard_map/ppermute | solution.py:30
  36.3 1.5 %along_rows.1.mix = f32[8192,128]{1,0:T(8,128)S(1)} custom-call(bf16[576,128]{1,0:T(8,128)(2,1)S(1)} %join.3.refs_0_, bf16[576,128]{1,0:T(8,128)(2,1)S(1)} %collective-permute-done.14.refs_1_, bf16[512,384]{1,0:T(8,128)(2,1)S(1)} %get-tuple-element.33.refs_2_, bf16[512,384]{1,0:T(8,128)(2,1)S(1)} %get-tuple-element.34.refs_3_, f32[5376,128]{1,0:T(8,128)S(1)} %wide.1.refs_4_, ...), custom_call_target="tpu_custom_call" | custom-call | tf_op jit(solution)/shard_map/along_rows/pallas_call | solution.py:412
  37.9 7.6 %picked.1.rows = f32[8192,128]{1,0:T(8,128)S(1)} custom-call(f32[8192,128]{1,0:T(8,128)S(1)} %along_rows.1.mix, s32[8192]{0:T(1024)S(1)} %and_or_fusion.where), custom_call_target="tpu_custom_call" | custom-call | tf_op jit(solution)/shard_map/picked/pallas_call | solution.py:486
  45.5 1.3 %sampled.1 = f32[1,8192]{1,0:T(1,128)S(1)} custom-call(f32[8192,128]{1,0:T(8,128)S(1)} %picked.1.rows, bf16[128,8192]{1,0:T(8,128)(2,1)S(1)} %signs.1), custom_call_target="tpu_custom_call" | custom-call | tf_op jit(solution)/shard_map/sampled/pallas_call | solution.py:513
  46.8 0.1 collective-permute-start.16
  46.9 1.2 %collective-permute-done.16 = f32[1,8192]{1,0:T(1,128)S(1)} collective-permute-done((f32[1,8192]{1,0:T(1,128)S(1)}, f32[1,8192]{1,0:T(1,128)S(1)}, u32[]{:S(2)}, u32[]{:S(2)}) %collective-permute-start.16) | collective-permute-done | bytes 32800 | tf_op jit(solution)/shard_map/ppermute | solution.py:30
  48.1 1.9 %collective-permute-start.17 = (f32[1,8192]{1,0:T(1,128)S(1)}, f32[1,8192]{1,0:T(1,128)S(1)}, u32[]{:S(2)}, u32[]{:S(2)}) collective-permute-start(f32[1,8192]{1,0:T(1,128)S(1)} %add.15), channel_id=1, source_target_pairs={{1,8},{3,10},{5,12},{7,14},{9,0},{11,2},{13,4},{15,6},{0,9},{2,11}... | collective-permute-start | bytes 98312 | tf_op jit(solution)/shard_map/ppermute | solution.py:273
  49.9 1.8 %collective-permute-start.18 = (f32[1,8192]{1,0:T(1,128)S(1)}, f32[1,8192]{1,0:T(1,128)S(1)}, u32[]{:S(2)}, u32[]{:S(2)}) collective-permute-start(f32[1,8192]{1,0:T(1,128)S(1)} %add.15), channel_id=1, source_target_pairs={{1,2},{3,0},{5,6},{7,4},{9,10},{11,8},{13,14},{15,12},{0,11},{2,9}... | collective-permute-start | bytes 98312 | tf_op jit(solution)/shard_map/ppermute | solution.py:273
  51.8 0.0 collective-permute-start.19
  51.8 3.1 %collective-permute-start.20 = (f32[1,8192]{1,0:T(1,128)S(1)}, f32[1,8192]{1,0:T(1,128)S(1)}, u32[]{:S(2)}, u32[]{:S(2)}) collective-permute-start(f32[1,8192]{1,0:T(1,128)S(1)} %add.15), channel_id=1, source_target_pairs={{1,6},{3,4},{5,2},{7,0},{9,14},{11,12},{13,10},{15,8},{0,15},{2,13... | collective-permute-start | bytes 98312 | tf_op jit(solution)/shard_map/ppermute | solution.py:273
  54.9 0.0 collective-permute-done.17
  54.9 0.0 collective-permute-done.18
  54.9 0.2 collective-permute-done.19
  55.1 1.4 %collective-permute-done.20 = f32[1,8192]{1,0:T(1,128)S(1)} collective-permute-done((f32[1,8192]{1,0:T(1,128)S(1)}, f32[1,8192]{1,0:T(1,128)S(1)}, u32[]{:S(2)}, u32[]{:S(2)}) %collective-permute-start.20) | collective-permute-done | bytes 32800 | tf_op jit(solution)/shard_map/ppermute | solution.py:273
  56.5 0.1 fusion.1
  56.6 1.5 %collective-permute-start.21 = (f32[1,8192]{1,0:T(1,128)S(1)}, f32[1,8192]{1,0:T(1,128)S(1)}, u32[]{:S(2)}, u32[]{:S(2)}) collective-permute-start(f32[1,8192]{1,0:T(1,128)S(1)} %fusion.1), channel_id=1, source_target_pairs={{0,1},{1,0},{2,3},{3,2},{4,5},{5,4},{6,7},{7,6},{8,9},{9,8},{10,11... | collective-permute-start | bytes 98312 | tf_op jit(solution)/shard_map/ppermute | solution.py:30
  58.1 0.9 %collective-permute-done.21 = f32[1,8192]{1,0:T(1,128)S(1)} collective-permute-done((f32[1,8192]{1,0:T(1,128)S(1)}, f32[1,8192]{1,0:T(1,128)S(1)}, u32[]{:S(2)}, u32[]{:S(2)}) %collective-permute-start.21) | collective-permute-done | bytes 32800 | tf_op jit(solution)/shard_map/ppermute | solution.py:30
  59.0 0.6 %add.19 = f32[1,8192]{1,0:T(1,128)} add(f32[1,8192]{1,0:T(1,128)S(1)} %fusion.1, f32[1,8192]{1,0:T(1,128)S(1)} %collective-permute-done.21) | non-fusion elementwise | flops 8192 | bytes 98304 | tf_op jit(solution)/shard_map/add | solution.py:277
  (8 shorter events, 0.2 us)
Async XLA Ops:
  1.9 6.9 %collective-permute-start = (bf16[576,128]{1,0:T(8,128)(2,1)S(1)}, bf16[576,128]{1,0:T(8,128)(2,1)S(1)}, u32[]{:S(2)}, u32[]{:S(2)}) collective-permute-start(bf16[576,128]{1,0:T(8,128)(2,1)S(1)} %get-tuple-element.36), channel_id=1, source_target_pairs={{0,2},{2,0},{4,6},{6,4},{8,10},{10,8},{12,14},{14,12},{1,3},{3,1},... | collective-permute-start | bytes 442376 | tf_op jit(solution)/shard_map/ppermute | solution.py:30
  8.2 21.0 %copy-start.1 = (s32[8192]{0:T(1024)S(1)}, s32[8192]{0:T(1024)}, u32[]{:S(2)}) copy-start(s32[8192]{0:T(1024)} %param.25) | copy-start | bytes 98308
  8.2 5.4 %collective-permute-start.7 = (bf16[576,128]{1,0:T(8,128)(2,1)S(1)}, bf16[576,128]{1,0:T(8,128)(2,1)S(1)}, u32[]{:S(2)}, u32[]{:S(2)}) collective-permute-start(bf16[576,128]{1,0:T(8,128)(2,1)S(1)} %get-tuple-element.45), channel_id=1, source_target_pairs={{0,2},{2,0},{4,6},{6,4},{8,10},{10,8},{12,14},{14,12},{1,3},{3,1},... | collective-permute-start | bytes 442376 | tf_op jit(solution)/shard_map/ppermute | solution.py:30
  8.9 8.4 %collective-permute-start.1 = (bf16[144,128]{1,0:T(8,128)(2,1)S(1)}, bf16[144,128]{1,0:T(8,128)(2,1)S(1)}, u32[]{:S(2)}, u32[]{:S(2)}) collective-permute-start(bf16[144,128]{1,0:T(8,128)(2,1)S(1)} %get-tuple-element.38), channel_id=1, source_target_pairs={{0,12},{2,14},{4,8},{6,10},{8,4},{10,6},{12,0},{14,2},{1,13},{3,15... | collective-permute-start | bytes 110600 | tf_op jit(solution)/shard_map/ppermute | solution.py:30
  12.7 5.3 %collective-permute-start.2 = (bf16[144,128]{1,0:T(8,128)(2,1)S(1)}, bf16[144,128]{1,0:T(8,128)(2,1)S(1)}, u32[]{:S(2)}, u32[]{:S(2)}) collective-permute-start(bf16[144,128]{1,0:T(8,128)(2,1)S(1)} %get-tuple-element.39), channel_id=1, source_target_pairs={{0,8},{2,10},{4,12},{6,14},{8,0},{10,2},{12,4},{14,6},{1,9},{3,11}... | collective-permute-start | bytes 110600 | tf_op jit(solution)/shard_map/ppermute | solution.py:30
  12.7 5.3 %collective-permute-start.3 = (bf16[144,128]{1,0:T(8,128)(2,1)S(1)}, bf16[144,128]{1,0:T(8,128)(2,1)S(1)}, u32[]{:S(2)}, u32[]{:S(2)}) collective-permute-start(bf16[144,128]{1,0:T(8,128)(2,1)S(1)} %get-tuple-element.40), channel_id=1, source_target_pairs={{0,4},{2,6},{4,0},{6,2},{8,12},{10,14},{12,8},{14,10},{1,5},{3,7},... | collective-permute-start | bytes 110600 | tf_op jit(solution)/shard_map/ppermute | solution.py:30
  13.5 19.3 %copy-start = (s32[1048576]{0:T(1024)S(1)}, s32[1048576]{0:T(1024)}, u32[]{:S(2)}) copy-start(s32[1048576]{0:T(1024)} %param.24) | copy-start | bytes 12582916
  13.6 8.2 %collective-permute-start.10 = (bf16[144,128]{1,0:T(8,128)(2,1)S(1)}, bf16[144,128]{1,0:T(8,128)(2,1)S(1)}, u32[]{:S(2)}, u32[]{:S(2)}) collective-permute-start(bf16[144,128]{1,0:T(8,128)(2,1)S(1)} %get-tuple-element.50), channel_id=1, source_target_pairs={{0,12},{2,14},{4,8},{6,10},{8,4},{10,6},{12,0},{14,2},{1,13},{3,15... | collective-permute-start | bytes 110600 | tf_op jit(solution)/shard_map/ppermute | solution.py:30
  17.3 5.3 %collective-permute-start.8 = (bf16[144,128]{1,0:T(8,128)(2,1)S(1)}, bf16[144,128]{1,0:T(8,128)(2,1)S(1)}, u32[]{:S(2)}, u32[]{:S(2)}) collective-permute-start(bf16[144,128]{1,0:T(8,128)(2,1)S(1)} %get-tuple-element.48), channel_id=1, source_target_pairs={{0,8},{2,10},{4,12},{6,14},{8,0},{10,2},{12,4},{14,6},{1,9},{3,11}... | collective-permute-start | bytes 110600 | tf_op jit(solution)/shard_map/ppermute | solution.py:30
  17.3 5.3 %collective-permute-start.9 = (bf16[144,128]{1,0:T(8,128)(2,1)S(1)}, bf16[144,128]{1,0:T(8,128)(2,1)S(1)}, u32[]{:S(2)}, u32[]{:S(2)}) collective-permute-start(bf16[144,128]{1,0:T(8,128)(2,1)S(1)} %get-tuple-element.49), channel_id=1, source_target_pairs={{0,4},{2,6},{4,0},{6,2},{8,12},{10,14},{12,8},{14,10},{1,5},{3,7},... | collective-permute-start | bytes 110600 | tf_op jit(solution)/shard_map/ppermute | solution.py:30
  18.1 8.2 %collective-permute-start.4 = (bf16[144,128]{1,0:T(8,128)(2,1)S(1)}, bf16[144,128]{1,0:T(8,128)(2,1)S(1)}, u32[]{:S(2)}, u32[]{:S(2)}) collective-permute-start(bf16[144,128]{1,0:T(8,128)(2,1)S(1)} %add_up.5.own), channel_id=1, source_target_pairs={{0,12},{2,14},{4,8},{6,10},{8,4},{10,6},{12,0},{14,2},{1,13},{3,15... | collective-permute-start | bytes 110600 | tf_op jit(solution)/shard_map/ppermute | solution.py:30
  21.8 5.5 %collective-permute-start.5 = (bf16[144,128]{1,0:T(8,128)(2,1)S(1)}, bf16[144,128]{1,0:T(8,128)(2,1)S(1)}, u32[]{:S(2)}, u32[]{:S(2)}) collective-permute-start(bf16[144,128]{1,0:T(8,128)(2,1)S(1)} %add_up.5.own), channel_id=1, source_target_pairs={{0,8},{2,10},{4,12},{6,14},{8,0},{10,2},{12,4},{14,6},{1,9},{3,11}... | collective-permute-start | bytes 110600 | tf_op jit(solution)/shard_map/ppermute | solution.py:30
  21.8 5.5 %collective-permute-start.6 = (bf16[144,128]{1,0:T(8,128)(2,1)S(1)}, bf16[144,128]{1,0:T(8,128)(2,1)S(1)}, u32[]{:S(2)}, u32[]{:S(2)}) collective-permute-start(bf16[144,128]{1,0:T(8,128)(2,1)S(1)} %add_up.5.own), channel_id=1, source_target_pairs={{0,4},{2,6},{4,0},{6,2},{8,12},{10,14},{12,8},{14,10},{1,5},{3,7},... | collective-permute-start | bytes 110600 | tf_op jit(solution)/shard_map/ppermute | solution.py:30
  22.6 7.0 %collective-permute-start.11 = (bf16[144,128]{1,0:T(8,128)(2,1)S(1)}, bf16[144,128]{1,0:T(8,128)(2,1)S(1)}, u32[]{:S(2)}, u32[]{:S(2)}) collective-permute-start(bf16[144,128]{1,0:T(8,128)(2,1)S(1)} %add_up.7.own), channel_id=1, source_target_pairs={{0,12},{2,14},{4,8},{6,10},{8,4},{10,6},{12,0},{14,2},{1,13},{3,15... | collective-permute-start | bytes 110600 | tf_op jit(solution)/shard_map/ppermute | solution.py:30
  26.2 4.9 %collective-permute-start.12 = (bf16[144,128]{1,0:T(8,128)(2,1)S(1)}, bf16[144,128]{1,0:T(8,128)(2,1)S(1)}, u32[]{:S(2)}, u32[]{:S(2)}) collective-permute-start(bf16[144,128]{1,0:T(8,128)(2,1)S(1)} %add_up.7.own), channel_id=1, source_target_pairs={{0,8},{2,10},{4,12},{6,14},{8,0},{10,2},{12,4},{14,6},{1,9},{3,11}... | collective-permute-start | bytes 110600 | tf_op jit(solution)/shard_map/ppermute | solution.py:30
  26.2 4.9 %collective-permute-start.13 = (bf16[144,128]{1,0:T(8,128)(2,1)S(1)}, bf16[144,128]{1,0:T(8,128)(2,1)S(1)}, u32[]{:S(2)}, u32[]{:S(2)}) collective-permute-start(bf16[144,128]{1,0:T(8,128)(2,1)S(1)} %add_up.7.own), channel_id=1, source_target_pairs={{0,4},{2,6},{4,0},{6,2},{8,12},{10,14},{12,8},{14,10},{1,5},{3,7},... | collective-permute-start | bytes 110600 | tf_op jit(solution)/shard_map/ppermute | solution.py:30
  27.3 5.4 %collective-permute-start.15 = (bf16[576,128]{1,0:T(8,128)(2,1)S(1)}, bf16[576,128]{1,0:T(8,128)(2,1)S(1)}, u32[]{:S(2)}, u32[]{:S(2)}) collective-permute-start(bf16[576,128]{1,0:T(8,128)(2,1)S(1)} %join.2.refs_0_), channel_id=1, source_target_pairs={{0,2},{2,0},{4,6},{6,4},{8,10},{10,8},{12,14},{14,12},{1,3},{3,1},... | collective-permute-start | bytes 442376 | tf_op jit(solution)/shard_map/ppermute | solution.py:30
  31.1 5.2 %collective-permute-start.14 = (bf16[576,128]{1,0:T(8,128)(2,1)S(1)}, bf16[576,128]{1,0:T(8,128)(2,1)S(1)}, u32[]{:S(2)}, u32[]{:S(2)}) collective-permute-start(bf16[576,128]{1,0:T(8,128)(2,1)S(1)} %join.3.refs_0_), channel_id=1, source_target_pairs={{0,2},{2,0},{4,6},{6,4},{8,10},{10,8},{12,14},{14,12},{1,3},{3,1},... | collective-permute-start | bytes 442376 | tf_op jit(solution)/shard_map/ppermute | solution.py:30
  46.8 1.3 %collective-permute-start.16 = (f32[1,8192]{1,0:T(1,128)S(1)}, f32[1,8192]{1,0:T(1,128)S(1)}, u32[]{:S(2)}, u32[]{:S(2)}) collective-permute-start(f32[1,8192]{1,0:T(1,128)S(1)} %sampled.1), channel_id=1, source_target_pairs={{0,1},{1,0},{2,3},{3,2},{4,5},{5,4},{6,7},{7,6},{8,9},{9,8},{10,11... | collective-permute-start | bytes 98312 | tf_op jit(solution)/shard_map/ppermute | solution.py:30
  48.1 6.8 %collective-permute-start.17 = (f32[1,8192]{1,0:T(1,128)S(1)}, f32[1,8192]{1,0:T(1,128)S(1)}, u32[]{:S(2)}, u32[]{:S(2)}) collective-permute-start(f32[1,8192]{1,0:T(1,128)S(1)} %add.15), channel_id=1, source_target_pairs={{1,8},{3,10},{5,12},{7,14},{9,0},{11,2},{13,4},{15,6},{0,9},{2,11}... | collective-permute-start | bytes 98312 | tf_op jit(solution)/shard_map/ppermute | solution.py:273
  49.9 5.0 %collective-permute-start.18 = (f32[1,8192]{1,0:T(1,128)S(1)}, f32[1,8192]{1,0:T(1,128)S(1)}, u32[]{:S(2)}, u32[]{:S(2)}) collective-permute-start(f32[1,8192]{1,0:T(1,128)S(1)} %add.15), channel_id=1, source_target_pairs={{1,2},{3,0},{5,6},{7,4},{9,10},{11,8},{13,14},{15,12},{0,11},{2,9}... | collective-permute-start | bytes 98312 | tf_op jit(solution)/shard_map/ppermute | solution.py:273
  51.8 3.3 %collective-permute-start.19 = (f32[1,8192]{1,0:T(1,128)S(1)}, f32[1,8192]{1,0:T(1,128)S(1)}, u32[]{:S(2)}, u32[]{:S(2)}) collective-permute-start(f32[1,8192]{1,0:T(1,128)S(1)} %add.15), channel_id=1, source_target_pairs={{1,4},{3,6},{5,0},{7,2},{9,12},{11,14},{13,8},{15,10},{0,13},{2,15... | collective-permute-start | bytes 98312 | tf_op jit(solution)/shard_map/ppermute | solution.py:273
  51.8 4.7 %collective-permute-start.20 = (f32[1,8192]{1,0:T(1,128)S(1)}, f32[1,8192]{1,0:T(1,128)S(1)}, u32[]{:S(2)}, u32[]{:S(2)}) collective-permute-start(f32[1,8192]{1,0:T(1,128)S(1)} %add.15), channel_id=1, source_target_pairs={{1,6},{3,4},{5,2},{7,0},{9,14},{11,12},{13,10},{15,8},{0,15},{2,13... | collective-permute-start | bytes 98312 | tf_op jit(solution)/shard_map/ppermute | solution.py:273
  56.6 2.4 %collective-permute-start.21 = (f32[1,8192]{1,0:T(1,128)S(1)}, f32[1,8192]{1,0:T(1,128)S(1)}, u32[]{:S(2)}, u32[]{:S(2)}) collective-permute-start(f32[1,8192]{1,0:T(1,128)S(1)} %fusion.1), channel_id=1, source_target_pairs={{0,1},{1,0},{2,3},{3,2},{4,5},{5,4},{6,7},{7,6},{8,9},{9,8},{10,11... | collective-permute-start | bytes 98312 | tf_op jit(solution)/shard_map/ppermute | solution.py:30
